TPU v7x, 128 devices: a whole 4x4x4 slice. The times are simulated.
128 devices in a mesh: subj: 4 (over y_lo, core), tile: 32 (over x, y_hi, z).
Axes of the slice: x: 4, y: 4 (y_hi: 2, y_lo: 2; y = y_hi * 2 + y_lo), z: 4, core: 2. Of those that a mesh axis runs over, the one named last changes fastest.
Arguments:
- template: float32 [8, 64, 256, 256], P(None, None, 'tile'), may hold values from -6 to 6
- images: float32 [32, 64, 256, 256], P('subj', None, 'tile'), may hold values from -6 to 6
- velocity: int32 [32, 3, 64, 256, 256], P('subj', None, None, 'tile'), may hold values from -2048 to 2047
- groups: int32 [32], P('subj'), may hold values from 0 to 7
Outputs:
- gradient: float32 [8, 64, 256, 256], P('subj', None, 'tile')
All inputs are finite; a program needn't handle non-finite values.
Results may differ from a plain program's by a relative error of at most 0.00007.
Values sent between devices are 32-bit elements; how exact they have to be, the bound alone decides.
No kernel may reach another device: no remote copies, remote signals or barrier semaphores. Data moves between devices by JAX's collectives and lax.ppermute only.
A program may use at most 256 MiB of HBM per device.

v0:
```python
import jax
import jax.numpy as jnp
from jax import lax
from jax.sharding import PartitionSpec as P

UPWIND_POS = (1.0 / 6.0, -1.0, 0.5, 1.0 / 3.0, 0.0)
UPWIND_NEG = (0.0, -1.0 / 3.0, -0.5, 1.0, -1.0 / 6.0)
VELOCITY_UNIT = 1.0 / 8192.0


def extended(cells, sides, width):
    for axis, dim in sides:
        count = lax.axis_size(axis)
        ends = count - 1
        head = lax.slice_in_dim(cells, 0, width, axis=dim)
        tail = lax.slice_in_dim(cells, cells.shape[dim] - width, cells.shape[dim], axis=dim)
        cells = jnp.concatenate(
            [
                lax.ppermute(tail, axis, [(i, (i + 1) % count) for i in range(ends)]),
                cells,
                lax.ppermute(head, axis, [((i + 1) % count, i) for i in range(ends)]),
            ],
            axis=dim,
        )
    return cells


def pad_along(field, along):
    widths = [(0, 0)] * field.ndim
    widths[along] = (2, 2)
    return jnp.pad(field, widths)


def stencil_valid(field, along, coeffs):
    length = field.shape[along] - 4
    result = coeffs[0] * lax.slice_in_dim(field, 0, length, axis=along)
    for shift in range(1, 5):
        result = result + coeffs[shift] * lax.slice_in_dim(field, shift, shift + length, axis=along)
    return result


def stencil_transpose(field, along, coeffs):
    length = field.shape[along] - 4
    result = coeffs[0] * lax.slice_in_dim(field, 4, 4 + length, axis=along)
    for shift in range(1, 5):
        result = result + coeffs[shift] * lax.slice_in_dim(
            field, 4 - shift, 4 - shift + length, axis=along
        )
    return result


def advance(moved_ext, speeds):
    offset = moved_ext.ndim - 3
    row_axis = offset + 1
    length = moved_ext.shape[row_axis] - 4
    middle = lax.slice_in_dim(moved_ext, 2, 2 + length, axis=row_axis)
    result = middle
    for component in range(3):
        along = offset + component
        forward_part = jnp.maximum(speeds[component], 0.0)
        backward_part = jnp.minimum(speeds[component], 0.0)
        source = moved_ext if component == 1 else pad_along(middle, along)
        result = result - forward_part * stencil_valid(source, along, UPWIND_POS)
        result = result - backward_part * stencil_valid(source, along, UPWIND_NEG)
    return result


def retreat(adjoint_mid, flux_pos, flux_neg, speeds):
    offset = adjoint_mid.ndim - 3
    result = adjoint_mid - stencil_transpose(flux_pos, offset + 1, UPWIND_POS)
    result = result - stencil_transpose(flux_neg, offset + 1, UPWIND_NEG)
    for component in (0, 2):
        along = offset + component
        forward_part = jnp.maximum(speeds[component], 0.0)
        backward_part = jnp.minimum(speeds[component], 0.0)
        result = result - stencil_transpose(
            pad_along(forward_part * adjoint_mid, along), along, UPWIND_POS
        )
        result = result - stencil_transpose(
            pad_along(backward_part * adjoint_mid, along), along, UPWIND_NEG
        )
    return result


def shards(template, images, velocity, groups):
    speed_all = velocity.astype(jnp.float32) * VELOCITY_UNIT
    speeds = (speed_all[:, 0], speed_all[:, 1], speed_all[:, 2])
    onehot = (groups[:, None] == jnp.arange(template.shape[0], dtype=jnp.int32)[None, :]).astype(
        jnp.float32
    )
    initial = jnp.einsum("sg,gxyz->sxyz", onehot, template, precision=lax.Precision.HIGHEST)
    moved = initial
    for substep in range(2):
        moved_ext = extended(moved, (("tile", 2),), 2)
        moved = advance(moved_ext, speeds)
    adjoint = moved - images
    for substep in range(2):
        pieces = jnp.stack(
            (jnp.maximum(speeds[1], 0.0) * adjoint, jnp.minimum(speeds[1], 0.0) * adjoint)
        )
        padded_flux = extended(pieces, (("tile", 3),), 2)
        adjoint = retreat(adjoint, padded_flux[0], padded_flux[1], speeds)
    partial_sums = jnp.einsum("sg,sxyz->gxyz", onehot, adjoint, precision=lax.Precision.HIGHEST)
    return lax.psum_scatter(partial_sums, "subj", scatter_dimension=0, tiled=True)


def solution(mesh):
    in_specs = (
        P(None, None, "tile", None),
        P("subj", None, "tile", None),
        P("subj", None, None, "tile", None),
        P("subj"),
    )
    out_specs = P("subj", None, "tile", None)
    return jax.shard_map(shards, mesh=mesh, in_specs=in_specs, out_specs=out_specs, check_vma=False)
```

profile of v0, /device:TPU:2, one launch (start us, length us, event | category | flops | bytes accessed | tf_op | source)
XLA Modules:
  0.0 443.0 jit_solution(15801659395533294386)
XLA Ops:
  6.5 6.6 %fusion.93 = f32[8,64,8,256]{3,0,2,1:T(8,128)S(1)} fusion(f32[8,64,8,256]{3,2,1,0:T(8,128)} %param.4, s32[8]{0:T(128)} %param.7), kind=kOutput, calls=%fused_computation.166 | convolution fusion | flops 100663360 | bytes 8388640 | tf_op jit(solution)/shard_map/sg,gxyz->sxyz/dot_general | solution.py:91
  13.1 1.5 fusion.158
  14.7 3.8 collective-permute-start
  18.5 6.8 %collective-permute-start.1 = (f32[8,64,2,256]{3,0,2,1:T(8,128)}, f32[8,64,2,256]{3,0,2,1:T(8,128)S(1)}, u32[]{:S(2)}, u32[]{:S(2)}) collective-permute-start(f32[8,64,2,256]{3,0,2,1:T(8,128)} %get-tuple-element.30), channel_id=1, source_target_pairs={{1,0},{2,1},{3,2},{4,3},{5,4},{6,5},{7,6},{8,7},{9,8},{10,9},{11,1... | collective-permute-start | bytes 3145736 | tf_op jit(solution)/shard_map/ppermute | solution.py:21
  25.3 17.2 %fusion = f32[8,3,64,8,256]{4,0,3,2,1:T(8,128)} fusion(s32[8,3,64,8,256]{4,3,2,1,0:T(8,128)} %param.6), kind=kLoop, calls=%fused_computation.3 | loop fusion | flops 6291456 | bytes 25165824 | tf_op jit(solution)/shard_map/mul | solution.py:86
  42.5 4.1 collective-permute-done
  46.6 1.3 collective-permute-done.1
  47.9 11.5 %fusion.76 = f32[8,64,8,256]{3,0,2,1:T(8,128)S(1)} fusion(f32[8,64,8,256]{3,0,2,1:T(8,128)S(1)} %fusion.93, f32[8,64,2,256]{3,0,2,1:T(8,128)S(1)} %collective-permute-done.1, f32[8,64,2,256]{3,0,2,1:T(8,128)S(1)} %collective-permute-done, f32[8,3,64,8,256]{4,0,3,2,1:T(8,128)} %fusion), kind=kLoop, calls=%fused_computation.129 | loop fusion | flops 72351744 | bytes 23068672 | tf_op jit(solution)/shard_map/sub | solution.py:64
  59.6 1.9 collective-permute-start.2
  61.5 9.0 %collective-permute-start.3 = (f32[8,64,2,256]{3,0,2,1:T(8,128)S(1)}, f32[8,64,2,256]{3,0,2,1:T(8,128)S(1)}, u32[]{:S(2)}, u32[]{:S(2)}) collective-permute-start(f32[8,64,2,256]{3,0,2,1:T(8,128)S(1)} %get-tuple-element.28), channel_id=1, source_target_pairs={{1,0},{2,1},{3,2},{4,3},{5,4},{6,5},{7,6},{8,7},{9,8},{10,9},{11,1... | collective-permute-start | bytes 3145736 | tf_op jit(solution)/shard_map/ppermute | solution.py:21
  70.5 20.1 %collective-permute-done.2 = f32[8,64,2,256]{3,0,2,1:T(8,128)S(1)} collective-permute-done((f32[8,64,2,256]{3,0,2,1:T(8,128)S(1)}, f32[8,64,2,256]{3,0,2,1:T(8,128)S(1)}, u32[]{:S(2)}, u32[]{:S(2)}) %collective-permute-start.2) | collective-permute-done | bytes 1048608 | tf_op jit(solution)/shard_map/ppermute | solution.py:19
  90.7 1.2 collective-permute-done.3
  91.8 35.3 %bitcast_multiply_fusion.21 = (f32[8,64,8,256]{3,0,2,1:T(8,128)}, f32[8,64,8,256]{3,0,2,1:T(8,128)S(1)}) fusion(f32[8,3,64,8,256]{4,0,3,2,1:T(8,128)} %fusion, f32[8,64,8,256]{3,2,1,0:T(8,128)} %param.5, f32[8,64,8,256]{3,0,2,1:T(8,128)} %copy-done.2, f32[8,64,2,256]{3,0,2,1:T(8,128)S(1)} %collective-permute-done.3, ...), kind=kLoop, calls=%fused_computation.161 | loop fusion | flops 74448896 | bytes 31457280 | tf_op jit(solution)/shard_map/mul | solution.py:77
  127.1 10.5 %fusion.87 = (f32[1,8,64,8,256]{4,1,3,2,0:T(8,128)S(1)}, f32[8,64,8,256]{3,0,2,1:T(8,128)}, f32[8,64,8,256]{3,0,2,1:T(8,128)}, f32[8,64,8,256]{3,0,2,1:T(8,128)}, f32[1,8,64,8,256]{4,1,3,2,0:T(8,128)S(1)}) fusion(f32[8,64,8,256]{3,0,2,1:T(8,128)S(1)} %get-tuple-element.8, f32[8,3,64,8,256]{4,0,3,2,1:T(8,128)} %fusion), kind=kLoop, calls=%fused_computation.152 | loop fusion | flops 10485760 | bytes 37748736 | tf_op jit(solution)/shard_map/stack | solution.py:98
  138.1 1.9 collective-permute-start.4
  140.0 8.9 %collective-permute-start.5 = (f32[2,8,64,2,256]{4,1,3,2,0:T(8,128)S(1)}, f32[2,8,64,2,256]{4,1,3,2,0:T(8,128)S(1)}, u32[]{:S(2)}, u32[]{:S(2)}) collective-permute-start(f32[2,8,64,2,256]{4,1,3,2,0:T(8,128)S(1)} %get-tuple-element.26), channel_id=1, source_target_pairs={{1,0},{2,1},{3,2},{4,3},{5,4},{6,5},{7,6},{8,7},{9,8},{10,9},{11,1... | collective-permute-start | bytes 6291464 | tf_op jit(solution)/shard_map/ppermute | solution.py:21
  148.9 41.9 %collective-permute-done.4 = f32[2,8,64,2,256]{4,1,3,2,0:T(8,128)S(1)} collective-permute-done((f32[2,8,64,2,256]{4,1,3,2,0:T(8,128)S(1)}, f32[2,8,64,2,256]{4,1,3,2,0:T(8,128)S(1)}, u32[]{:S(2)}, u32[]{:S(2)}) %collective-permute-start.4) | collective-permute-done | bytes 2097184 | tf_op jit(solution)/shard_map/ppermute | solution.py:19
  190.8 1.2 collective-permute-done.5
  192.0 5.0 %pad_maximum_fusion = f32[2,8,64,12,256]{4,1,3,2,0:T(8,128)} fusion(f32[2,8,64,2,256]{4,1,3,2,0:T(8,128)S(1)} %collective-permute-done.5, f32[1,8,64,8,256]{4,1,3,2,0:T(8,128)S(1)} %get-tuple-element.18, f32[1,8,64,8,256]{4,1,3,2,0:T(8,128)S(1)} %get-tuple-element.14, f32[2,8,64,2,256]{4,1,3,2,0:T(8,128)S(1)} %collective-permute-done.4), kind=kLoop, calls=%fused_computation | loop fusion | flops 9437184 | bytes 25165824 | tf_op jit(solution)/shard_map/concatenate | solution.py:17
  197.0 11.0 %slice_bitcast_fusion.3 = (f32[8,64,12,256]{3,0,2,1:T(8,128)}, f32[8,64,12,256]{3,0,2,1:T(8,128)}) fusion(f32[2,8,64,12,256]{4,1,3,2,0:T(8,128)} %pad_maximum_fusion), kind=kLoop, calls=%fused_computation.31 | loop fusion | bytes 25165824 | tf_op jit(solution)/shard_map/squeeze | solution.py:102
  208.0 45.5 %bitcast_multiply_fusion.20 = (f32[8,64,8,256]{3,0,2,1:T(8,128)}, f32[8,64,8,256]{3,0,2,1:T(8,128)}) fusion(f32[8,3,64,8,256]{4,0,3,2,1:T(8,128)} %fusion, f32[8,64,8,256]{3,0,2,1:T(8,128)} %get-tuple-element.17, f32[8,64,8,256]{3,0,2,1:T(8,128)} %get-tuple-element.15, f32[8,64,8,256]{3,0,2,1:T(8,128)} %get-tuple-element.16, ...), kind=kLoop, calls=%fused_computation.160 | loop fusion | flops 61865984 | bytes 75497472 | tf_op jit(solution)/shard_map/mul | solution.py:77
  253.6 8.3 %bitcast_multiply_fusion.16 = (f32[8,64,8,256]{3,0,2,1:T(8,128)}, f32[8,64,8,256]{3,0,2,1:T(8,128)}, f32[8,64,8,256]{3,0,2,1:T(8,128)}, f32[1,8,64,8,256]{4,1,3,2,0:T(8,128)S(1)}, f32[1,8,64,8,256]{4,1,3,2,0:T(8,128)}) fusion(f32[8,64,8,256]{3,0,2,1:T(8,128)} %get-tuple-element.6, f32[8,3,64,8,256]{4,0,3,2,1:T(8,128)S(1)} %bitcast.117), kind=kLoop, calls=%fused_computation.154 | loop fusion | flops 10485760 | bytes 37748736 | tf_op jit(solution)/shard_map/mul | solution.py:80
  261.9 2.2 pad_maximum_fusion.7
  264.1 1.9 collective-permute-start.6
  266.0 9.2 %collective-permute-start.7 = (f32[2,8,64,2,256]{4,1,3,2,0:T(8,128)S(1)}, f32[2,8,64,2,256]{4,1,3,2,0:T(8,128)S(1)}, u32[]{:S(2)}, u32[]{:S(2)}) collective-permute-start(f32[2,8,64,2,256]{4,1,3,2,0:T(8,128)S(1)} %get-tuple-element.24), channel_id=1, source_target_pairs={{1,0},{2,1},{3,2},{4,3},{5,4},{6,5},{7,6},{8,7},{9,8},{10,9},{11,1... | collective-permute-start | bytes 6291464 | tf_op jit(solution)/shard_map/ppermute | solution.py:21
  275.2 40.7 %collective-permute-done.6 = f32[2,8,64,2,256]{4,1,3,2,0:T(8,128)S(1)} collective-permute-done((f32[2,8,64,2,256]{4,1,3,2,0:T(8,128)S(1)}, f32[2,8,64,2,256]{4,1,3,2,0:T(8,128)S(1)}, u32[]{:S(2)}, u32[]{:S(2)}) %collective-permute-start.6) | collective-permute-done | bytes 2097184 | tf_op jit(solution)/shard_map/ppermute | solution.py:19
  315.9 1.2 collective-permute-done.7
  317.1 5.0 %pad_maximum_fusion.1 = f32[2,8,64,12,256]{4,1,3,2,0:T(8,128)} fusion(f32[2,8,64,2,256]{4,1,3,2,0:T(8,128)S(1)} %collective-permute-done.7, f32[1,8,64,8,256]{4,1,3,2,0:T(8,128)S(1)} %get-tuple-element.12, f32[1,8,64,8,256]{4,1,3,2,0:T(8,128)S(1)} %copy-done.1, f32[2,8,64,2,256]{4,1,3,2,0:T(8,128)S(1)} %collective-permute-done.6), kind=kLoop, calls=%fused_computation.1 | loop fusion | flops 9437184 | bytes 25165824 | tf_op jit(solution)/shard_map/concatenate | solution.py:17
  322.1 10.8 %slice_bitcast_fusion.1 = (f32[8,64,12,256]{3,0,2,1:T(8,128)}, f32[8,64,12,256]{3,0,2,1:T(8,128)}) fusion(f32[2,8,64,12,256]{4,1,3,2,0:T(8,128)} %pad_maximum_fusion.1), kind=kLoop, calls=%fused_computation.29 | loop fusion | bytes 25165824 | tf_op jit(solution)/shard_map/squeeze | solution.py:102
  332.9 49.5 %fusion.29 = f32[8,64,8,256]{3,0,2,1:T(8,128)} fusion(f32[8,64,8,256]{3,0,2,1:T(8,128)} %get-tuple-element.10, f32[8,64,8,256]{3,0,2,1:T(8,128)} %get-tuple-element.11, f32[8,64,12,256]{3,0,2,1:T(8,128)} %get-tuple-element.20, f32[8,64,8,256]{3,0,2,1:T(8,128)} %get-tuple-element.6, f32[8,64,12,256]{3,0,2,1:T(8,128)} %get-tuple-element.19, ...), kind=kOutput, calls=%fused_computation.68 | convolution fusion | flops 160432192 | bytes 67108896 | tf_op jit(solution)/shard_map/sg,sxyz->gxyz/dot_general | solution.py:103
  382.3 5.6 %copy.14 = f32[8,64,8,256]{3,2,1,0:T(8,128)} copy(f32[8,64,8,256]{3,0,2,1:T(8,128)} %fusion.29) | data formatting | bytes 8388608 | tf_op jit(solution)/shard_map/sg,sxyz->gxyz/dot_general | solution.py:103
  387.9 48.2 %reduce-scatter.2.cloned.1.call-done = f32[2,64,8,256]{3,2,1,0:T(8,128)} async-done(((f32[8,64,8,256]{3,2,1,0:T(8,128)}), f32[2,64,8,256]{3,2,1,0:T(8,128)}) %reduce-scatter.2.cloned.1.call-update) | async-done | bytes 1048592 | tf_op jit(solution)/shard_map/reduce_scatter | solution.py:104
  (19 shorter events, 0.7 us)
Async XLA Ops:
  6.5 429.6 %reduce-scatter.2.cloned.1.call-start = ((), (), s32[]{:S(2)}) async-start(), calls=%async_computation.1 | async-start | bytes 5242880 | tf_op jit(solution)/shard_map/reduce_scatter | solution.py:104
  14.7 31.9 %collective-permute-start = (f32[8,64,2,256]{3,0,2,1:T(8,128)}, f32[8,64,2,256]{3,0,2,1:T(8,128)S(1)}, u32[]{:S(2)}, u32[]{:S(2)}) collective-permute-start(f32[8,64,2,256]{3,0,2,1:T(8,128)} %get-tuple-element.29), channel_id=1, source_target_pairs={{0,1},{1,2},{2,3},{3,4},{4,5},{5,6},{6,7},{7,8},{8,9},{9,10},{10,1... | collective-permute-start | bytes 3145736 | tf_op jit(solution)/shard_map/ppermute | solution.py:19
  18.5 29.4 %collective-permute-start.1 = (f32[8,64,2,256]{3,0,2,1:T(8,128)}, f32[8,64,2,256]{3,0,2,1:T(8,128)S(1)}, u32[]{:S(2)}, u32[]{:S(2)}) collective-permute-start(f32[8,64,2,256]{3,0,2,1:T(8,128)} %get-tuple-element.30), channel_id=1, source_target_pairs={{1,0},{2,1},{3,2},{4,3},{5,4},{6,5},{7,6},{8,7},{9,8},{10,9},{11,1... | collective-permute-start | bytes 3145736 | tf_op jit(solution)/shard_map/ppermute | solution.py:21
  59.4 31.3 %copy-start.2 = (f32[8,64,8,256]{3,0,2,1:T(8,128)}, f32[8,64,8,256]{3,0,2,1:T(8,128)S(1)}, u32[]{:S(2)}) copy-start(f32[8,64,8,256]{3,0,2,1:T(8,128)S(1)} %fusion.76) | copy-start | bytes 12582916
  59.6 31.1 %collective-permute-start.2 = (f32[8,64,2,256]{3,0,2,1:T(8,128)S(1)}, f32[8,64,2,256]{3,0,2,1:T(8,128)S(1)}, u32[]{:S(2)}, u32[]{:S(2)}) collective-permute-start(f32[8,64,2,256]{3,0,2,1:T(8,128)S(1)} %get-tuple-element.27), channel_id=1, source_target_pairs={{0,1},{1,2},{2,3},{3,4},{4,5},{5,6},{6,7},{7,8},{8,9},{9,10},{10,1... | collective-permute-start | bytes 3145736 | tf_op jit(solution)/shard_map/ppermute | solution.py:19
  61.5 30.3 %collective-permute-start.3 = (f32[8,64,2,256]{3,0,2,1:T(8,128)S(1)}, f32[8,64,2,256]{3,0,2,1:T(8,128)S(1)}, u32[]{:S(2)}, u32[]{:S(2)}) collective-permute-start(f32[8,64,2,256]{3,0,2,1:T(8,128)S(1)} %get-tuple-element.28), channel_id=1, source_target_pairs={{1,0},{2,1},{3,2},{4,3},{5,4},{6,5},{7,6},{8,7},{9,8},{10,9},{11,1... | collective-permute-start | bytes 3145736 | tf_op jit(solution)/shard_map/ppermute | solution.py:21
  127.1 10.5 %copy-start = (f32[8,64,8,256]{3,0,2,1:T(8,128)}, f32[8,64,8,256]{3,0,2,1:T(8,128)S(1)}, u32[]{:S(2)}) copy-start(f32[8,64,8,256]{3,0,2,1:T(8,128)S(1)} %get-tuple-element.8) | copy-start | bytes 12582916
  138.1 52.7 %collective-permute-start.4 = (f32[2,8,64,2,256]{4,1,3,2,0:T(8,128)S(1)}, f32[2,8,64,2,256]{4,1,3,2,0:T(8,128)S(1)}, u32[]{:S(2)}, u32[]{:S(2)}) collective-permute-start(f32[2,8,64,2,256]{4,1,3,2,0:T(8,128)S(1)} %get-tuple-element.25), channel_id=1, source_target_pairs={{0,1},{1,2},{2,3},{3,4},{4,5},{5,6},{6,7},{7,8},{8,9},{9,10},{10,1... | collective-permute-start | bytes 6291464 | tf_op jit(solution)/shard_map/ppermute | solution.py:19
  140.0 52.0 %collective-permute-start.5 = (f32[2,8,64,2,256]{4,1,3,2,0:T(8,128)S(1)}, f32[2,8,64,2,256]{4,1,3,2,0:T(8,128)S(1)}, u32[]{:S(2)}, u32[]{:S(2)}) collective-permute-start(f32[2,8,64,2,256]{4,1,3,2,0:T(8,128)S(1)} %get-tuple-element.26), channel_id=1, source_target_pairs={{1,0},{2,1},{3,2},{4,3},{5,4},{6,5},{7,6},{8,7},{9,8},{10,9},{11,1... | collective-permute-start | bytes 6291464 | tf_op jit(solution)/shard_map/ppermute | solution.py:21
  197.0 56.6 %slice-start = ((s8[12582912]{0:T(1024)(128)(4,1)}), s8[4194304]{0:T(1024)(128)(4,1)S(1)}, s32[]{:S(2)}) async-start(s8[12582912]{0:T(1024)(128)(4,1)} %bitcast.116), calls=%async_computation.2 | async-start | bytes 8388608
  208.0 45.6 %slice-start.1 = ((s8[12582912]{0:T(1024)(128)(4,1)}), s8[4194304]{0:T(1024)(128)(4,1)S(1)}, s32[]{:S(2)}) async-start(s8[12582912]{0:T(1024)(128)(4,1)} %bitcast.116), calls=%async_computation.3 | async-start | bytes 8388608
  208.0 45.6 %slice-start.2 = ((s8[12582912]{0:T(1024)(128)(4,1)}), s8[4194304]{0:T(1024)(128)(4,1)S(1)}, s32[]{:S(2)}) async-start(s8[12582912]{0:T(1024)(128)(4,1)} %bitcast.116), calls=%async_computation.4 | async-start | bytes 8388608
  261.9 55.2 %copy-start.1 = (f32[1,8,64,8,256]{4,1,3,2,0:T(8,128)S(1)}, f32[1,8,64,8,256]{4,1,3,2,0:T(8,128)}, u32[]{:S(2)}) copy-start(f32[1,8,64,8,256]{4,1,3,2,0:T(8,128)} %get-tuple-element.13) | copy-start | bytes 12582916
  264.1 51.8 %collective-permute-start.6 = (f32[2,8,64,2,256]{4,1,3,2,0:T(8,128)S(1)}, f32[2,8,64,2,256]{4,1,3,2,0:T(8,128)S(1)}, u32[]{:S(2)}, u32[]{:S(2)}) collective-permute-start(f32[2,8,64,2,256]{4,1,3,2,0:T(8,128)S(1)} %get-tuple-element.23), channel_id=1, source_target_pairs={{0,1},{1,2},{2,3},{3,4},{4,5},{5,6},{6,7},{7,8},{8,9},{9,10},{10,1... | collective-permute-start | bytes 6291464 | tf_op jit(solution)/shard_map/ppermute | solution.py:19
  266.0 51.1 %collective-permute-start.7 = (f32[2,8,64,2,256]{4,1,3,2,0:T(8,128)S(1)}, f32[2,8,64,2,256]{4,1,3,2,0:T(8,128)S(1)}, u32[]{:S(2)}, u32[]{:S(2)}) collective-permute-start(f32[2,8,64,2,256]{4,1,3,2,0:T(8,128)S(1)} %get-tuple-element.24), channel_id=1, source_target_pairs={{1,0},{2,1},{3,2},{4,3},{5,4},{6,5},{7,6},{8,7},{9,8},{10,9},{11,1... | collective-permute-start | bytes 6291464 | tf_op jit(solution)/shard_map/ppermute | solution.py:21
  322.1 10.8 %copy-start.3 = (s32[8]{0:T(128)S(1)}, s32[8]{0:T(128)}, u32[]{:S(2)}) copy-start(s32[8]{0:T(128)} %param.7) | copy-start | bytes 100
Sparse Core Ops, SparseCore 0:
  388.1 48.0 reduce-scatter.1
where the time goes:
time: 444 us; the launch traced here: 443 us
  waiting for transfers between devices  160 us (36%)
  other arithmetic  141 us (32%)
  matrix products  56 us (13%)
  starting transfers between devices  43.5 us (10%)
  local copies, waits for them, and re-layouts  29.1 us (7%)
  between operations  13.6 us (3%)
    ppermute x4, waiting for transfers between devices, extended(): lax.ppermute(tail, axis, [(i, (i + 1) % count) for i in range(ends)])  107 us
    mul x2, other arithmetic, retreat(): forward_part * adjoint_mid  80.8 us
    dot_general x1, matrix products, shards(): jnp.einsum('sg,sxyz->gxyz', onehot, adjoint, precision=lax.Precision.HIGH...  49.5 us
    reduce_scatter x1, waiting for transfers between devices, shards(): lax.psum_scatter(partial_sums, 'subj', scatter_dimension=0, tiled=True)  48.2 us
    ppermute x4, starting transfers between devices, extended(): lax.ppermute(head, axis, [((i + 1) % count, i) for i in range(ends)])  33.9 us
    squeeze x2, local copies, waits for them, and re-layouts, shards(): adjoint = retreat(adjoint, padded_flux[0], padded_flux[1], speeds)  21.8 us
    mul x1, other arithmetic, shards(): speed_all = velocity.astype(jnp.float32) * VELOCITY_UNIT  17.2 us
    sub x1, other arithmetic, advance(): result = result - backward_part * stencil_valid(source, along, UPWIND_NEG)  11.5 us
  transfers between devices with their start and end apart: 9, of which 9 were waited for; matrix products, arithmetic and copies ran while one was open for 4% of the time, Pallas kernels for 0%

commit v1 on v0

v1 whole, which is shorter than its diff:
```python
import functools

import jax
import jax.numpy as jnp
from jax import lax
from jax.experimental import pallas as pl
from jax.experimental.pallas import tpu as pltpu
from jax.sharding import PartitionSpec as P

SCALE = 1.0 / (6.0 * 8192.0)
SX = 64
ROWS = 8
NZ = 256
HALF = 128
SUBS = 8
GROUPS = 8
CUTS = (36,)
VMEM = 48 * 1024 * 1024
UNROLL = 4


def bounds(shift):
    return [0] + [cut - shift for cut in CUTS] + [SX]


def spec(shape, index):
    return pl.BlockSpec(tuple(pl.Element(size) for size in shape), index)


def lanes(value, shift, lane):
    low, high = value[:, :HALF], value[:, HALF:]
    roll_low, roll_high = pltpu.roll(low, shift % HALF, 1), pltpu.roll(high, shift % HALF, 1)
    if shift > 0:
        mask = lane < shift
        first = jnp.where(mask, 0.0, roll_low)
        second = jnp.where(mask, roll_low, roll_high)
    else:
        mask = lane >= HALF + shift
        first = jnp.where(mask, roll_high, roll_low)
        second = jnp.where(mask, 0.0, roll_high)
    return jnp.concatenate([first, second], axis=1)


def rows(value, shift):
    return pltpu.roll(value, shift % ROWS, 0)


def iotas():
    row = lax.broadcasted_iota(jnp.int32, (ROWS, NZ), 0)
    lane = lax.broadcasted_iota(jnp.int32, (ROWS, HALF), 1)
    return row, lane


def frame(upper, lower):
    return jnp.concatenate([upper, jnp.zeros((ROWS - 4, NZ), jnp.float32), lower], axis=0)


def upwind(speed, back2, back1, mid3, fore1, fore2):
    speed = speed.astype(jnp.float32)
    forward = speed > 0.0
    near = jnp.where(forward, back1, fore1)
    far = jnp.where(forward, back2, fore2)
    ahead = jnp.where(forward, fore1, back1)
    return jnp.abs(speed) * (far - 6.0 * near + mid3 + (ahead + ahead))


def advance_slice(get, x, halo, speed, masks):
    row, lane = masks
    zero = jnp.zeros((ROWS, NZ), jnp.float32)

    def at(position):
        value = get(position)
        return zero if value is None else value

    mid = get(x)
    mid3 = 3.0 * mid
    change = upwind(speed[0], at(x - 2), at(x - 1), mid3, at(x + 1), at(x + 2))
    back1 = rows(jnp.where(row == 7, halo, mid), 1)
    back2 = rows(jnp.where(row >= 6, halo, mid), 2)
    fore1 = rows(jnp.where(row == 0, halo, mid), -1)
    fore2 = rows(jnp.where(row <= 1, halo, mid), -2)
    change = change + upwind(speed[1], back2, back1, mid3, fore1, fore2)
    back1, back2 = lanes(mid, 1, lane), lanes(mid, 2, lane)
    fore1, fore2 = lanes(mid, -1, lane), lanes(mid, -2, lane)
    change = change + upwind(speed[2], back2, back1, mid3, fore1, fore2)
    return mid - SCALE * change


def parts(speed, twice):
    speed = speed.astype(jnp.float32)
    pos = jnp.maximum(speed, 0.0) * twice
    neg = jnp.minimum(speed, 0.0) * twice
    pos3, neg3 = 3.0 * pos, 3.0 * neg
    return 0.5 * pos, -(pos3 + neg), pos - neg, pos + neg3, -0.5 * neg


def scatter_rows(speed, twice, row):
    plus2, plus1, middle, minus1, minus2 = parts(speed, twice)
    step = rows(plus2, -1)
    out_far = step[7:8]
    step = rows(plus1 + jnp.where(row < 7, step, 0.0), -1)
    out_near = step[7:8]
    change = jnp.where(row < 7, step, 0.0)
    step = rows(minus2, 1)
    in_far = step[0:1]
    step = rows(minus1 + jnp.where(row > 0, step, 0.0), 1)
    in_near = step[0:1]
    change = change + jnp.where(row > 0, step, 0.0)
    return change, middle, (out_far, out_near), (in_near, in_far)


def scatter_lanes(speed, twice, lane):
    plus2, plus1, middle, minus1, minus2 = parts(speed, twice)
    change = lanes(plus1 + lanes(plus2, -1, lane), -1, lane)
    change = change + lanes(minus1 + lanes(minus2, 1, lane), 1, lane)
    return change, middle


def loop(start, stop, body, carry):
    whole = (stop - start) // UNROLL

    def several(step, carry):
        for k in range(UNROLL):
            carry = body(start + step * UNROLL + k, carry)
        return carry

    if whole > 0:
        carry = lax.fori_loop(0, whole, several, carry)
    for x in range(start + whole * UNROLL, stop):
        carry = body(x, carry)
    return carry


def getter(main, main_low, main_high, tail=None, tail_low=0):
    def get(x):
        if isinstance(x, int):
            if x < 0 or x >= SX:
                return None
            if x < main_low:
                return tail[0, x - tail_low]
        return main[0, x - main_low]

    return get


def walk(low, high, main_low, main_high, body):
    first = min(max(low, main_low + 2), high)
    last = max(min(high, main_high - 2), first)
    for x in range(low, first):
        body(x, 0)
    loop(first, last, lambda x, carry: (body(x, carry), carry)[1], 0)
    for x in range(last, high):
        body(x, 0)


def first_kernel(low, high, in_low, in_high, groups, side, template, prev_own, prev_other, next_own, next_other,
                 velocity, moved, up, down):
    masks = iotas()
    own = (groups[pl.program_id(0)] // (GROUPS // 2)) == side[0]
    get = getter(template, in_low, in_high)

    def body(x, carry):
        k = x - low
        upper = jnp.where(own, next_own[0, k], next_other[0, k])
        lower = jnp.where(own, prev_own[0, k], prev_other[0, k])
        speed = [velocity[0, d, k] for d in range(3)]
        value = advance_slice(get, x, frame(upper, lower), speed, masks)
        moved[0, k] = value
        up[0, k] = value[0:2]
        down[0, k] = value[6:8]

    walk(low, high, in_low, in_high, body)


def second_kernel(low, high, in_low, in_high, tail_low, *refs):
    if tail_low is None:
        moved, prev, next_, velocity, images, residual, up, down = refs
        tail = None
    else:
        tail, moved, prev, next_, velocity, images, residual, up, down = refs
    masks = iotas()
    get = getter(moved, in_low, in_high, tail, tail_low)

    def body(x, carry):
        k = x - low
        speed = [velocity[0, d, k] for d in range(3)]
        value = advance_slice(get, x, frame(next_[0, k], prev[0, k]), speed, masks)
        value = value - images[0, k]
        residual[0, k] = value
        _, _, out, into = scatter_rows(speed[1], value + value, masks[0])
        up[0, k, 0:1] = out[0]
        up[0, k, 1:2] = out[1]
        down[0, k, 0:1] = into[0]
        down[0, k, 1:2] = into[1]

    walk(low, high, in_low, in_high, body)


def scatter_walk(low, high, get, speed_of, extra, emit, edges, masks, loop_low):
    zero = jnp.zeros((ROWS, NZ), jnp.float32)
    row, lane = masks

    def body(x, carry, inside=True, last=True):
        now0, now1, now2, now3 = carry
        value = get(x)
        twice = value + value
        speed = speed_of(x)
        plus2, plus1, middle, minus1, minus2 = parts(speed[0], twice)
        if not isinstance(x, int) or x >= low + 2:
            done = get(x - 2) - SCALE * (now0 + plus2)
            emit(x - 2, done)
        if inside:
            ychange, ymiddle, out, into = scatter_rows(speed[1], twice, row)
            zchange, zmiddle = scatter_lanes(speed[2], twice, lane)
            own = (ychange + zchange) + 1.5 * (middle + ymiddle + zmiddle)
            if extra is not None:
                own = own + extra(x)
            if edges is not None:
                edges(x, out, into)
            now2 = now2 + own
        return now1 + plus1, now2, now3 + minus1, minus2

    carry = (zero,) * 4
    start = max(low - 2, 0)
    stop = min(high + 2, SX)
    first = min(max(loop_low, low + 2), high)
    for x in range(start, first):
        carry = body(x, carry, inside=low <= x < high)
    carry = loop(first, high, body, carry)
    for x in range(high, stop):
        carry = body(x, carry, inside=False)
    if high == SX:
        for x, change in ((SX - 2, carry[0]), (SX - 1, carry[1])):
            emit(x, get(x) - SCALE * change)


def third_kernel(low3, high3, low4, high4, in_low, vel_low, tail_low, keep_low, groups, side, *refs):
    refs = list(refs)
    tail = before = None
    if tail_low is not None:
        tail, before = refs[:2]
        refs = refs[2:]
    main, prev, next_, velocity, sums, edges = refs[:6]
    refs = refs[6:]
    keep = refs.pop(0) if keep_low is not None else None
    (adjoint,) = refs
    masks = iotas()
    s = pl.program_id(0)
    group = groups[s]
    owner = group // 2
    core = (owner % 2 == side[0]).astype(jnp.int32)
    slot = core * 4 + (owner // 2 == side[1]).astype(jnp.int32) * 2 + group % 2

    @pl.when(s == 0)
    def clear():
        sums[...] = jnp.zeros_like(sums)
        edges[...] = jnp.zeros_like(edges)

    get = getter(main, in_low, SX, tail, tail_low)
    base = low4 - 2 if low4 > 0 else 0
    if before is not None:
        for x in range(base, low3):
            adjoint[0, x - base] = before[0, x - base]

    def speed_of(x):
        return [velocity[0, d, x - vel_low] for d in range(3)]

    def extra(x):
        k = x - low3
        upper = prev[0, k]
        lower = next_[0, k]
        return frame(upper, lower)

    def emit(x, value):
        adjoint[0, x - base] = value

    scatter_walk(low3, high3, get, speed_of, extra, emit, None, masks, in_low + 2)
    if keep is not None:
        for x in range(keep_low, high3):
            keep[0, x - keep_low] = adjoint[0, x - base]

    def emit_sum(x, value):
        k = x - low4
        sums[slot, k] = sums[slot, k] + value

    def emit_edges(x, out, into):
        k = x - low4
        block = jnp.concatenate([out[0], out[1], into[0], into[1]], axis=0)
        edges[slot, k] = edges[slot, k] - SCALE * block

    get4 = getter(adjoint, base, SX)
    scatter_walk(low4, high4, get4, speed_of, None, emit_sum, emit_edges, masks, low4 + 2)


def call(body, grid, scalars, ins, outs, arrays, scratch=(), flops=0):
    nbytes = sum(a.size * 4 for a in arrays)
    return pl.pallas_call(
        body,
        grid_spec=pltpu.PrefetchScalarGridSpec(
            num_scalar_prefetch=len(scalars),
            grid=grid,
            in_specs=ins,
            out_specs=[o[1] for o in outs],
            scratch_shapes=list(scratch),
        ),
        out_shape=[jax.ShapeDtypeStruct(o[0], jnp.float32) for o in outs],
        compiler_params=pltpu.CompilerParams(vmem_limit_bytes=VMEM, dimension_semantics=("arbitrary",)),
        cost_estimate=pl.CostEstimate(flops=flops, bytes_accessed=nbytes, transcendentals=0),
    )(*scalars, *arrays)


def subject(*tail):
    return lambda s, *scalars: (s,) + tail


def neighbours(up, down, count):
    from_next = lax.ppermute(up, "tile", [(i + 1, i) for i in range(count - 1)])
    from_prev = lax.ppermute(down, "tile", [(i, i + 1) for i in range(count - 1)])
    return from_prev, from_next


def shards(template, images, velocity, groups):
    count = lax.axis_size("tile")
    place = lax.axis_index("subj")
    core, high_y = place % 2, place // 2
    half = GROUPS // 2
    core_pairs = [(0, 1), (1, 0), (2, 3), (3, 2)]
    y_pairs = [(0, 2), (2, 0), (1, 3), (3, 1)]
    side = jnp.stack([core, high_y]).astype(jnp.int32)
    chunks = len(CUTS) + 1

    mine = lax.dynamic_slice_in_dim(template, core * half, half, axis=0)
    prev_own, next_own = neighbours(mine[:, :, 0:2], mine[:, :, 6:8], count)
    both = lax.ppermute(jnp.stack([prev_own, next_own]), "subj", core_pairs)
    prev_other, next_other = both[0], both[1]

    field = lambda n: (SUBS, n, ROWS, NZ)
    edge = lambda n: (SUBS, n, 2, NZ)

    b1, b2, b3, b4 = (bounds(2 * k) for k in range(4))
    moved, moved_edges = [], []
    for c in range(chunks):
        low, high = b1[c], b1[c + 1]
        n = high - low
        in_low, in_high = max(low - 2, 0), min(high + 2, SX)
        halo_spec = spec((1, n, 2, NZ), lambda s, g, d, low=low: (g[s] % half, low, 0, 0))
        out = call(
            functools.partial(first_kernel, low, high, in_low, in_high),
            (SUBS,),
            (groups, side),
            [spec((1, in_high - in_low, ROWS, NZ), lambda s, g, d, in_low=in_low: (g[s], in_low, 0, 0))]
            + [halo_spec] * 4
            + [spec((1, 3, n, ROWS, NZ), subject(0, low, 0, 0))],
            [(field(n), spec((1, n, ROWS, NZ), subject(0, 0, 0)))]
            + [(edge(n), spec((1, n, 2, NZ), subject(0, 0, 0)))] * 2,
            (template, prev_own, prev_other, next_own, next_other, velocity),
            flops=50 * SUBS * n * ROWS * NZ,
        )
        moved.append(out[0])
        moved_edges.append(neighbours(out[1], out[2], count))

    residual, residual_edges = [], []
    for c in range(chunks):
        low, high = b2[c], b2[c + 1]
        n = high - low
        main_low, main_high = b1[c], b1[c + 1]
        m = main_high - main_low
        ins, arrays, tail_low = [], (), None
        if c > 0:
            tail_low = main_low - 4
            before_low = b1[c - 1]
            ins.append(spec((1, 4, ROWS, NZ), subject(tail_low - before_low, 0, 0)))
            arrays += (moved[c - 1],)
        prev, next_ = moved_edges[c]
        if c > 0:
            back = main_low - low
            prev = jnp.concatenate([moved_edges[c - 1][0][:, -back:], prev], axis=1)
            next_ = jnp.concatenate([moved_edges[c - 1][1][:, -back:], next_], axis=1)
        ins += [
            spec((1, m, ROWS, NZ), subject(0, 0, 0)),
            spec((1, n, 2, NZ), subject(0, 0, 0)),
            spec((1, n, 2, NZ), subject(0, 0, 0)),
            spec((1, 3, n, ROWS, NZ), subject(0, low, 0, 0)),
            spec((1, n, ROWS, NZ), subject(low, 0, 0)),
        ]
        arrays += (moved[c], prev, next_, velocity, images)
        out = call(
            functools.partial(second_kernel, low, high, main_low, main_high, tail_low),
            (SUBS,),
            (),
            ins,
            [(field(n), spec((1, n, ROWS, NZ), subject(0, 0, 0)))]
            + [(edge(n), spec((1, n, 2, NZ), subject(0, 0, 0)))] * 2,
            arrays,
            flops=60 * SUBS * n * ROWS * NZ,
        )
        residual.append(out[0])
        residual_edges.append(neighbours(out[1], out[2], count))

    results, kept = [], None
    for c in range(chunks):
        low3, high3, low4, high4 = b3[c], b3[c + 1], b4[c], b4[c + 1]
        n3, n4 = high3 - low3, high4 - low4
        main_low, main_high = b2[c], b2[c + 1]
        m = main_high - main_low
        ins, arrays, tail_low = [], (), None
        prev, next_ = residual_edges[c]
        if c > 0:
            tail_low = main_low - 4
            ins.append(spec((1, 4, ROWS, NZ), subject(tail_low - b2[c - 1], 0, 0)))
            ins.append(spec((1, 4, ROWS, NZ), subject(0, 0, 0)))
            arrays += (residual[c - 1], kept)
            back = main_low - low3
            prev = jnp.concatenate([residual_edges[c - 1][0][:, -back:], prev], axis=1)
            next_ = jnp.concatenate([residual_edges[c - 1][1][:, -back:], next_], axis=1)
        base = max(low4 - 2, 0)
        vel_low, vel_high = base, min(high3 + 2, SX)
        vn = vel_high - vel_low
        ins += [
            spec((1, m, ROWS, NZ), subject(0, 0, 0)),
            spec((1, n3, 2, NZ), subject(0, 0, 0)),
            spec((1, n3, 2, NZ), subject(0, 0, 0)),
            spec((1, 3, vn, ROWS, NZ), subject(0, vel_low, 0, 0)),
        ]
        arrays += (residual[c], prev, next_, velocity)
        outs = [
            ((GROUPS, n4, ROWS, NZ), spec((GROUPS, n4, ROWS, NZ), lambda s, *r: (0, 0, 0, 0))),
            ((GROUPS, n4, 4, NZ), spec((GROUPS, n4, 4, NZ), lambda s, *r: (0, 0, 0, 0))),
        ]
        keep_low = None
        if c + 1 < chunks:
            keep_low = high4 - 2
            outs.append(((SUBS, 4, ROWS, NZ), spec((1, 4, ROWS, NZ), subject(0, 0, 0))))
        out = call(
            functools.partial(third_kernel, low3, high3, low4, high4, main_low, vel_low, tail_low, keep_low),
            (SUBS,),
            (groups, side),
            ins,
            outs,
            arrays,
            scratch=[pltpu.VMEM((1, high3 - base, ROWS, NZ), jnp.float32)],
            flops=130 * SUBS * n4 * ROWS * NZ,
        )
        if keep_low is not None:
            kept = out[2]
        sums, edges = out[0], out[1]
        sums4 = sums[half:] + lax.ppermute(sums[:half], "subj", core_pairs)
        edges4 = edges[half:] + lax.ppermute(edges[:half], "subj", core_pairs)
        sums2 = sums4[2:] + lax.ppermute(sums4[:2], "subj", y_pairs)
        edges2 = edges4[2:] + lax.ppermute(edges4[:2], "subj", y_pairs)
        from_prev, from_next = neighbours(edges2[:, :, 0:2], edges2[:, :, 2:4], count)
        middle = jnp.zeros((2, n4, ROWS - 4, NZ), jnp.float32)
        results.append(sums2 + jnp.concatenate([from_prev, middle, from_next], axis=2))
    return jnp.concatenate(results, axis=1)


def solution(mesh):
    in_specs = (
        P(None, None, "tile", None),
        P("subj", None, "tile", None),
        P("subj", None, None, "tile", None),
        P("subj"),
    )
    out_specs = P("subj", None, "tile", None)
    return jax.shard_map(shards, mesh=mesh, in_specs=in_specs, out_specs=out_specs, check_vma=False)
```

time: 444 us -> 225 us (0.51)
  other arithmetic: 141 us -> 3.69 us
  waiting for transfers between devices: 160 us -> 41.7 us
  Pallas kernels: 0 us -> 92.4 us
  matrix products: 56 us -> 0 us
  starting transfers between devices: 43.5 us -> 78.3 us
  local copies, waits for them, and re-layouts: 29.1 us -> 7.12 us
  between operations: 13.6 us -> 0.5 us
    mul x4 -> x0, other arithmetic: 106 us -> none  [the longest x2 80.8 us: retreat(): forward_part * adjoint_mid]
    pallas_call x0 -> x6, Pallas kernels: none -> 92.4 us  [call(): pl.pallas_call(body, grid_spec=pltpu.PrefetchScalarGridSpec(num_scalar_pr...]
    ppermute x8 -> x23, waiting for transfers between devices: 112 us -> 41.7 us  [the longest x2 14.7 us: shards(): sums2 = sums4[2:] + lax.ppermute(sums4[:2], 'subj', y_pairs)]
    dot_general x2 -> x0, matrix products: 56 us -> none  [the longest x1 49.5 us: shards(): jnp.einsum('sg,sxyz->gxyz', onehot, adjoint, precision=lax.Precision.HIGH...]
    reduce_scatter x1 -> x0, waiting for transfers between devices: 48.2 us -> none  [shards(): lax.psum_scatter(partial_sums, 'subj', scatter_dimension=0, tiled=True)]
    ppermute x8 -> x23, starting transfers between devices: 43.5 us -> 78.3 us  [the longest x7 59.2 us: neighbours(): from_next = lax.ppermute(up, 'tile', [(i + 1, i) for i in range(count - 1)])]
    squeeze x2 -> x1, local copies, waits for them, and re-layouts: 21.8 us -> 0.36 us  [shards(): prev_other, next_other = (both[0], both[1])]
    sub x1 -> x0, other arithmetic: 11.5 us -> none  [advance(): result = result - backward_part * stencil_valid(source, along, UPWIND_NEG)]
  transfers between devices with their start and end apart: 9 -> 23, of which waited for: 9 -> 6; matrix products, arithmetic and copies ran while one was open for 4% -> 1% of each run, Pallas kernels for 0% -> 36%
where the time goes in v1:
time: 225 us; the launch traced here: 224 us
  Pallas kernels  92.4 us (41%)
  starting transfers between devices  78.3 us (35%)
  waiting for transfers between devices  41.7 us (19%)
  local copies, waits for them, and re-layouts  7.12 us (3%)
  other arithmetic  3.69 us (2%)
    pallas_call x6, Pallas kernels, call(): pl.pallas_call(body, grid_spec=pltpu.PrefetchScalarGridSpec(num_scalar_pr...  92.4 us
    ppermute x7, starting transfers between devices, neighbours(): from_next = lax.ppermute(up, 'tile', [(i + 1, i) for i in range(count - 1)])  59.2 us
    ppermute x2, waiting for transfers between devices, shards(): sums2 = sums4[2:] + lax.ppermute(sums4[:2], 'subj', y_pairs)  14.7 us
    ppermute x7, starting transfers between devices, neighbours(): lax.ppermute(down, 'tile', [(i, i + 1) for i in range(count - 1)])  13.4 us
    ppermute x7, waiting for transfers between devices, neighbours(): from_next = lax.ppermute(up, 'tile', [(i + 1, i) for i in range(count - 1)])  9.25 us
    ppermute x7, waiting for transfers between devices, neighbours(): lax.ppermute(down, 'tile', [(i, i + 1) for i in range(count - 1)])  8.65 us
    ppermute x2, waiting for transfers between devices, shards(): edges2 = edges4[2:] + lax.ppermute(edges4[:2], 'subj', y_pairs)  6.51 us
  transfers between devices with their start and end apart: 23, of which 6 were waited for; matrix products, arithmetic and copies ran while one was open for 1% of the time, Pallas kernels for 36%

profile of v1, /device:TPU:2, one launch (start us, length us, event | category | flops | bytes accessed | tf_op | source)
XLA Modules:
  0.0 223.8 jit_solution(12201700949514878045)
XLA Ops:
  0.0 2.6 %constant_dynamic-slice_fusion.1 = (f32[4,64,2,256]{3,2,1,0:T(2,128)S(1)}, f32[4,64,2,256]{3,2,1,0:T(2,128)S(1)}) fusion(f32[8,64,8,256]{3,2,1,0:T(8,128)} %template.3, s32[]{:T(128)S(6)} %select_n.16, s32[]{:T(128)S(6)} %add.51), kind=kLoop, calls=%fused_computation.20 | loop fusion | bytes 2097160 | tf_op jit(solution)/shard_map/slice | solution.py:333
  2.6 8.5 %collective-permute-start.1 = (f32[4,64,2,256]{3,2,1,0:T(2,128)S(1)}, f32[4,64,2,256]{3,2,1,0:T(2,128)S(1)}, u32[]{:S(2)}, u32[]{:S(2)}) collective-permute-start(f32[4,64,2,256]{3,2,1,0:T(2,128)S(1)} %get-tuple-element.39), channel_id=1, source_target_pairs={{1,0},{2,1},{3,2},{4,3},{5,4},{6,5},{7,6},{8,7},{9,8},{10,9},{11,1... | collective-permute-start | bytes 1572872 | tf_op jit(solution)/shard_map/ppermute | solution.py:317
  11.1 1.9 collective-permute-start
  13.0 9.2 %collective-permute-done.1.next_own = f32[4,64,2,256]{3,2,1,0:T(2,128)S(1)} collective-permute-done((f32[4,64,2,256]{3,2,1,0:T(2,128)S(1)}, f32[4,64,2,256]{3,2,1,0:T(2,128)S(1)}, u32[]{:S(2)}, u32[]{:S(2)}) %collective-permute-start.1) | collective-permute-done | bytes 524320 | tf_op jit(solution)/shard_map/ppermute | solution.py:317
  22.3 8.6 %collective-permute-done.prev_own = f32[4,64,2,256]{3,2,1,0:T(2,128)S(1)} collective-permute-done((f32[4,64,2,256]{3,2,1,0:T(2,128)S(1)}, f32[4,64,2,256]{3,2,1,0:T(2,128)S(1)}, u32[]{:S(2)}, u32[]{:S(2)}) %collective-permute-start) | collective-permute-done | bytes 524320 | tf_op jit(solution)/shard_map/ppermute | solution.py:318
  31.6 2.6 %collective-permute-done.2 = f32[2,4,64,2,256]{4,3,2,1,0:T(2,128)S(1)} collective-permute-done((f32[2,4,64,2,256]{4,3,2,1,0:T(2,128)S(1)}, f32[2,4,64,2,256]{4,3,2,1,0:T(2,128)S(1)}, u32[]{:S(2)}, u32[]{:S(2)}) %collective-permute-start.2) | collective-permute-done | bytes 1048608 | tf_op jit(solution)/shard_map/ppermute | solution.py:334
  34.6 11.3 %shard_map.46 = (f32[8,36,8,256]{3,2,1,0:T(8,128)S(1)}, f32[8,36,2,256]{3,2,1,0:T(2,128)S(1)}, f32[8,36,2,256]{3,2,1,0:T(2,128)S(1)}) custom-call(s32[8]{0:T(128)S(1)} %copy-done.2, s32[2]{0:T(128)S(1)} %pad_add_fusion.side, f32[8,64,8,256]{3,2,1,0:T(8,128)} %template.3, f32[4,64,2,256]{3,2,1,0:T(2,128)S(1)} %collective-permute-done.prev_own, ...), custom_call_target="tpu_custom_call" | custom-call | flops 29491200 | bytes 18874368 | tf_op jit(solution)/shard_map/pallas_call | solution.py:297
  45.9 1.4 copy-done
  47.3 1.9 collective-permute-start.3
  49.2 8.4 %collective-permute-start.4 = (f32[8,36,2,256]{3,2,1,0:T(2,128)S(1)}, f32[8,36,2,256]{3,2,1,0:T(2,128)S(1)}, u32[]{:S(2)}, u32[]{:S(2)}) collective-permute-start(f32[8,36,2,256]{3,2,1,0:T(2,128)S(1)} %get-tuple-element.24), channel_id=1, source_target_pairs={{1,0},{2,1},{3,2},{4,3},{5,4},{6,5},{7,6},{8,7},{9,8},{10,9},{11,1... | collective-permute-start | bytes 1769480 | tf_op jit(solution)/shard_map/ppermute | solution.py:317
  57.7 9.6 %shard_map.49 = (f32[8,28,8,256]{3,2,1,0:T(8,128)S(1)}, f32[8,28,2,256]{3,2,1,0:T(2,128)S(1)}, f32[8,28,2,256]{3,2,1,0:T(2,128)S(1)}) custom-call(s32[8]{0:T(128)S(1)} %copy-done.2, s32[2]{0:T(128)S(1)} %pad_add_fusion.side, f32[8,64,8,256]{3,2,1,0:T(8,128)} %template.3, f32[4,64,2,256]{3,2,1,0:T(2,128)S(1)} %collective-permute-done.prev_own, ...), custom_call_target="tpu_custom_call" | custom-call | flops 22937600 | bytes 18874368 | tf_op jit(solution)/shard_map/pallas_call | solution.py:297
  67.3 1.9 collective-permute-start.13
  69.2 8.4 %collective-permute-start.14 = (f32[8,28,2,256]{3,2,1,0:T(2,128)S(1)}, f32[8,28,2,256]{3,2,1,0:T(2,128)S(1)}, u32[]{:S(2)}, u32[]{:S(2)}) collective-permute-start(f32[8,28,2,256]{3,2,1,0:T(2,128)S(1)} %get-tuple-element.33), channel_id=1, source_target_pairs={{1,0},{2,1},{3,2},{4,3},{5,4},{6,5},{7,6},{8,7},{9,8},{10,9},{11,1... | collective-permute-start | bytes 1376264 | tf_op jit(solution)/shard_map/ppermute | solution.py:317
  77.7 11.5 %shard_map.47 = (f32[8,34,8,256]{3,2,1,0:T(8,128)S(1)}, f32[8,34,2,256]{3,2,1,0:T(2,128)S(1)}, f32[8,34,2,256]{3,2,1,0:T(2,128)S(1)}) custom-call(f32[8,36,8,256]{3,2,1,0:T(8,128)} %copy-done, f32[8,36,2,256]{3,2,1,0:T(2,128)S(1)} %collective-permute-done.3.refs_1_, f32[8,36,2,256]{3,2,1,0:T(2,128)S(1)} %collective-permute-done.4.refs_2_, ...), custom_call_target="tpu_custom_call" | custom-call | flops 33423360 | bytes 20316160 | tf_op jit(solution)/shard_map/pallas_call | solution.py:297
  89.2 1.4 copy-done.1
  90.6 1.9 collective-permute-start.5
  92.5 8.4 %collective-permute-start.6 = (f32[8,34,2,256]{3,2,1,0:T(2,128)S(1)}, f32[8,34,2,256]{3,2,1,0:T(2,128)S(1)}, u32[]{:S(2)}, u32[]{:S(2)}) collective-permute-start(f32[8,34,2,256]{3,2,1,0:T(2,128)S(1)} %get-tuple-element.27), channel_id=1, source_target_pairs={{1,0},{2,1},{3,2},{4,3},{5,4},{6,5},{7,6},{8,7},{9,8},{10,9},{11,1... | collective-permute-start | bytes 1671176 | tf_op jit(solution)/shard_map/ppermute | solution.py:317
  101.4 10.3 %shard_map.50 = (f32[8,30,8,256]{3,2,1,0:T(8,128)S(1)}, f32[8,30,2,256]{3,2,1,0:T(2,128)S(1)}, f32[8,30,2,256]{3,2,1,0:T(2,128)S(1)}) custom-call(f32[8,36,8,256]{3,2,1,0:T(8,128)} %copy-done, f32[8,28,8,256]{3,2,1,0:T(8,128)S(1)} %get-tuple-element.31.refs_1_, f32[8,30,2,256]{3,2,1,0:T(2,128)S(1)} %pad_maximum_fusion.4.refs_2_, ...), custom_call_target="tpu_custom_call" | custom-call | flops 29491200 | bytes 21954560 | tf_op jit(solution)/shard_map/pallas_call | solution.py:297
  111.8 1.9 collective-permute-start.15
  113.7 8.4 %collective-permute-start.16 = (f32[8,30,2,256]{3,2,1,0:T(2,128)S(1)}, f32[8,30,2,256]{3,2,1,0:T(2,128)S(1)}, u32[]{:S(2)}, u32[]{:S(2)}) collective-permute-start(f32[8,30,2,256]{3,2,1,0:T(2,128)S(1)} %get-tuple-element.36), channel_id=1, source_target_pairs={{1,0},{2,1},{3,2},{4,3},{5,4},{6,5},{7,6},{8,7},{9,8},{10,9},{11,1... | collective-permute-start | bytes 1474568 | tf_op jit(solution)/shard_map/ppermute | solution.py:317
  122.2 23.5 %shard_map.48 = (f32[8,30,8,256]{3,2,1,0:T(8,128)S(1)}, f32[8,30,4,256]{3,2,1,0:T(4,128)S(1)}, f32[8,4,8,256]{3,2,1,0:T(8,128)S(1)}) custom-call(s32[8]{0:T(128)S(1)} %copy-done.2, s32[2]{0:T(128)S(1)} %pad_add_fusion.side, f32[8,34,8,256]{3,2,1,0:T(8,128)} %copy-done.1, f32[8,34,2,256]{3,2,1,0:T(2,128)S(1)} %collective-permute-done.5.refs_1_, ...), custom_call_target="tpu_custom_call" | custom-call | flops 63897600 | bytes 15925248 | tf_op jit(solution)/shard_map/pallas_call | solution.py:297
  146.3 26.2 %shard_map.51 = (f32[8,34,8,256]{3,2,1,0:T(8,128)}, f32[8,34,4,256]{3,2,1,0:T(4,128)S(1)}) custom-call(s32[8]{0:T(128)S(1)} %copy-done.2, s32[2]{0:T(128)S(1)} %pad_add_fusion.side, f32[8,34,8,256]{3,2,1,0:T(8,128)} %copy-done.1, f32[8,4,8,256]{3,2,1,0:T(8,128)S(1)} %get-tuple-element.30.refs_1_, f32[8,30,8,256]{3,2,1,0:T(8,128)S(1)} %get-tuple-element.34.refs_2_, ...), custom_call_target="tpu_custom_call" | custom-call | flops 72417280 | bytes 18087936 | tf_op jit(solution)/shard_map/pallas_call | solution.py:297
  175.8 1.6 collective-permute-start.20
  177.3 6.5 %collective-permute-done.10 = f32[2,30,4,256]{3,2,1,0:T(4,128)S(1)} collective-permute-done((f32[2,30,4,256]{3,2,1,0:T(4,128)S(1)}, f32[2,30,4,256]{3,2,1,0:T(4,128)S(1)}, u32[]{:S(2)}, u32[]{:S(2)}) %collective-permute-start.10) | collective-permute-done | bytes 245792 | tf_op jit(solution)/shard_map/ppermute | solution.py:450
  184.0 1.9 collective-permute-start.11
  186.0 8.4 %collective-permute-start.12 = (f32[2,30,2,256]{3,2,1,0:T(2,128)S(1)}, f32[2,30,2,256]{3,2,1,0:T(2,128)S(1)}, u32[]{:S(2)}, u32[]{:S(2)}) collective-permute-start(f32[2,30,2,256]{3,2,1,0:T(2,128)S(1)} %get-tuple-element.46), channel_id=1, source_target_pairs={{1,0},{2,1},{3,2},{4,3},{5,4},{6,5},{7,6},{8,7},{9,8},{10,9},{11,1... | collective-permute-start | bytes 368648 | tf_op jit(solution)/shard_map/ppermute | solution.py:317
  195.4 1.6 collective-permute-start.18
  197.2 1.9 collective-permute-start.21
  199.1 8.4 %collective-permute-start.22 = (f32[2,34,2,256]{3,2,1,0:T(2,128)S(1)}, f32[2,34,2,256]{3,2,1,0:T(2,128)S(1)}, u32[]{:S(2)}, u32[]{:S(2)}) collective-permute-start(f32[2,34,2,256]{3,2,1,0:T(2,128)S(1)} %get-tuple-element.44), channel_id=1, source_target_pairs={{1,0},{2,1},{3,2},{4,3},{5,4},{6,5},{7,6},{8,7},{9,8},{10,9},{11,1... | collective-permute-start | bytes 417800 | tf_op jit(solution)/shard_map/ppermute | solution.py:317
  207.6 4.8 %collective-permute-done.8 = f32[2,30,8,256]{3,2,1,0:T(8,128)S(1)} collective-permute-done((f32[2,30,8,256]{3,2,1,0:T(8,128)S(1)}, f32[2,30,8,256]{3,2,1,0:T(8,128)S(1)}, u32[]{:S(2)}, u32[]{:S(2)}) %collective-permute-start.8) | collective-permute-done | bytes 491552 | tf_op jit(solution)/shard_map/ppermute | solution.py:449
  212.6 9.9 %collective-permute-done.18 = f32[2,34,8,256]{3,2,1,0:T(8,128)S(1)} collective-permute-done((f32[2,34,8,256]{3,2,1,0:T(8,128)S(1)}, f32[2,34,8,256]{3,2,1,0:T(8,128)S(1)}, u32[]{:S(2)}, u32[]{:S(2)}) %collective-permute-start.18) | collective-permute-done | bytes 557088 | tf_op jit(solution)/shard_map/ppermute | solution.py:449
  222.7 1.1 pad_maximum_fusion.1
  (61 shorter events, 7.1 us)
Async XLA Ops:
  2.6 19.7 %collective-permute-start.1 = (f32[4,64,2,256]{3,2,1,0:T(2,128)S(1)}, f32[4,64,2,256]{3,2,1,0:T(2,128)S(1)}, u32[]{:S(2)}, u32[]{:S(2)}) collective-permute-start(f32[4,64,2,256]{3,2,1,0:T(2,128)S(1)} %get-tuple-element.39), channel_id=1, source_target_pairs={{1,0},{2,1},{3,2},{4,3},{5,4},{6,5},{7,6},{8,7},{9,8},{10,9},{11,1... | collective-permute-start | bytes 1572872 | tf_op jit(solution)/shard_map/ppermute | solution.py:317
  11.1 19.8 %collective-permute-start = (f32[4,64,2,256]{3,2,1,0:T(2,128)S(1)}, f32[4,64,2,256]{3,2,1,0:T(2,128)S(1)}, u32[]{:S(2)}, u32[]{:S(2)}) collective-permute-start(f32[4,64,2,256]{3,2,1,0:T(2,128)S(1)} %get-tuple-element.40), channel_id=1, source_target_pairs={{0,1},{1,2},{2,3},{3,4},{4,5},{5,6},{6,7},{7,8},{8,9},{9,10},{10,1... | collective-permute-start | bytes 1572872 | tf_op jit(solution)/shard_map/ppermute | solution.py:318
  30.9 3.7 %copy-start.2 = (s32[8]{0:T(128)S(1)}, s32[8]{0:T(128)}, u32[]{:S(2)}) copy-start(s32[8]{0:T(128)} %groups.7) | copy-start | bytes 100
  31.5 2.7 %collective-permute-start.2 = (f32[2,4,64,2,256]{4,3,2,1,0:T(2,128)S(1)}, f32[2,4,64,2,256]{4,3,2,1,0:T(2,128)S(1)}, u32[]{:S(2)}, u32[]{:S(2)}) collective-permute-start(f32[2,4,64,2,256]{4,3,2,1,0:T(2,128)S(1)} %pad_maximum_fusion), channel_id=1, source_target_pairs={{0,32},{32,0},{64,96},{96,64},{1,33},{33,1},{65,97},{97,65},{2,34}... | collective-permute-start | bytes 3145736 | tf_op jit(solution)/shard_map/ppermute | solution.py:334
  45.9 1.4 copy-start
  47.3 30.4 %collective-permute-start.3 = (f32[8,36,2,256]{3,2,1,0:T(2,128)S(1)}, f32[8,36,2,256]{3,2,1,0:T(2,128)S(1)}, u32[]{:S(2)}, u32[]{:S(2)}) collective-permute-start(f32[8,36,2,256]{3,2,1,0:T(2,128)S(1)} %get-tuple-element.23), channel_id=1, source_target_pairs={{0,1},{1,2},{2,3},{3,4},{4,5},{5,6},{6,7},{7,8},{8,9},{9,10},{10,1... | collective-permute-start | bytes 1769480 | tf_op jit(solution)/shard_map/ppermute | solution.py:318
  49.2 28.5 %collective-permute-start.4 = (f32[8,36,2,256]{3,2,1,0:T(2,128)S(1)}, f32[8,36,2,256]{3,2,1,0:T(2,128)S(1)}, u32[]{:S(2)}, u32[]{:S(2)}) collective-permute-start(f32[8,36,2,256]{3,2,1,0:T(2,128)S(1)} %get-tuple-element.24), channel_id=1, source_target_pairs={{1,0},{2,1},{3,2},{4,3},{5,4},{6,5},{7,6},{8,7},{9,8},{10,9},{11,1... | collective-permute-start | bytes 1769480 | tf_op jit(solution)/shard_map/ppermute | solution.py:317
  67.3 33.7 %collective-permute-start.13 = (f32[8,28,2,256]{3,2,1,0:T(2,128)S(1)}, f32[8,28,2,256]{3,2,1,0:T(2,128)S(1)}, u32[]{:S(2)}, u32[]{:S(2)}) collective-permute-start(f32[8,28,2,256]{3,2,1,0:T(2,128)S(1)} %get-tuple-element.32), channel_id=1, source_target_pairs={{0,1},{1,2},{2,3},{3,4},{4,5},{5,6},{6,7},{7,8},{8,9},{9,10},{10,1... | collective-permute-start | bytes 1376264 | tf_op jit(solution)/shard_map/ppermute | solution.py:318
  69.2 32.0 %collective-permute-start.14 = (f32[8,28,2,256]{3,2,1,0:T(2,128)S(1)}, f32[8,28,2,256]{3,2,1,0:T(2,128)S(1)}, u32[]{:S(2)}, u32[]{:S(2)}) collective-permute-start(f32[8,28,2,256]{3,2,1,0:T(2,128)S(1)} %get-tuple-element.33), channel_id=1, source_target_pairs={{1,0},{2,1},{3,2},{4,3},{5,4},{6,5},{7,6},{8,7},{9,8},{10,9},{11,1... | collective-permute-start | bytes 1376264 | tf_op jit(solution)/shard_map/ppermute | solution.py:317
  89.2 1.4 copy-start.1
  90.6 31.6 %collective-permute-start.5 = (f32[8,34,2,256]{3,2,1,0:T(2,128)S(1)}, f32[8,34,2,256]{3,2,1,0:T(2,128)S(1)}, u32[]{:S(2)}, u32[]{:S(2)}) collective-permute-start(f32[8,34,2,256]{3,2,1,0:T(2,128)S(1)} %get-tuple-element.26), channel_id=1, source_target_pairs={{0,1},{1,2},{2,3},{3,4},{4,5},{5,6},{6,7},{7,8},{8,9},{9,10},{10,1... | collective-permute-start | bytes 1671176 | tf_op jit(solution)/shard_map/ppermute | solution.py:318
  92.5 29.7 %collective-permute-start.6 = (f32[8,34,2,256]{3,2,1,0:T(2,128)S(1)}, f32[8,34,2,256]{3,2,1,0:T(2,128)S(1)}, u32[]{:S(2)}, u32[]{:S(2)}) collective-permute-start(f32[8,34,2,256]{3,2,1,0:T(2,128)S(1)} %get-tuple-element.27), channel_id=1, source_target_pairs={{1,0},{2,1},{3,2},{4,3},{5,4},{6,5},{7,6},{8,7},{9,8},{10,9},{11,1... | collective-permute-start | bytes 1671176 | tf_op jit(solution)/shard_map/ppermute | solution.py:317
  111.8 34.1 %collective-permute-start.15 = (f32[8,30,2,256]{3,2,1,0:T(2,128)S(1)}, f32[8,30,2,256]{3,2,1,0:T(2,128)S(1)}, u32[]{:S(2)}, u32[]{:S(2)}) collective-permute-start(f32[8,30,2,256]{3,2,1,0:T(2,128)S(1)} %get-tuple-element.35), channel_id=1, source_target_pairs={{0,1},{1,2},{2,3},{3,4},{4,5},{5,6},{6,7},{7,8},{8,9},{9,10},{10,1... | collective-permute-start | bytes 1474568 | tf_op jit(solution)/shard_map/ppermute | solution.py:318
  113.7 32.4 %collective-permute-start.16 = (f32[8,30,2,256]{3,2,1,0:T(2,128)S(1)}, f32[8,30,2,256]{3,2,1,0:T(2,128)S(1)}, u32[]{:S(2)}, u32[]{:S(2)}) collective-permute-start(f32[8,30,2,256]{3,2,1,0:T(2,128)S(1)} %get-tuple-element.36), channel_id=1, source_target_pairs={{1,0},{2,1},{3,2},{4,3},{5,4},{6,5},{7,6},{8,7},{9,8},{10,9},{11,1... | collective-permute-start | bytes 1474568 | tf_op jit(solution)/shard_map/ppermute | solution.py:317
  145.7 29.1 %collective-permute-start.9 = (f32[4,30,4,256]{3,2,1,0:T(4,128)S(1)}, f32[4,30,4,256]{3,2,1,0:T(4,128)S(1)}, u32[]{:S(2)}, u32[]{:S(2)}) collective-permute-start(f32[4,30,4,256]{3,2,1,0:T(4,128)S(1)} %slice.93), channel_id=1, source_target_pairs={{0,32},{32,0},{64,96},{96,64},{1,33},{33,1},{65,97},{97,65},{2,34}... | collective-permute-start | bytes 1474568 | tf_op jit(solution)/shard_map/ppermute | solution.py:448
  172.5 1.6 copy-start.3
  172.6 3.0 %collective-permute-start.19 = (f32[4,34,4,256]{3,2,1,0:T(4,128)S(1)}, f32[4,34,4,256]{3,2,1,0:T(4,128)S(1)}, u32[]{:S(2)}, u32[]{:S(2)}) collective-permute-start(f32[4,34,4,256]{3,2,1,0:T(4,128)S(1)} %slice.107), channel_id=1, source_target_pairs={{0,32},{32,0},{64,96},{96,64},{1,33},{33,1},{65,97},{97,65},{2,34}... | collective-permute-start | bytes 1671176 | tf_op jit(solution)/shard_map/ppermute | solution.py:448
  173.3 21.1 %collective-permute-start.7 = (f32[4,30,8,256]{3,2,1,0:T(8,128)S(1)}, f32[4,30,8,256]{3,2,1,0:T(8,128)S(1)}, u32[]{:S(2)}, u32[]{:S(2)}) collective-permute-start(f32[4,30,8,256]{3,2,1,0:T(8,128)S(1)} %slice.89), channel_id=1, source_target_pairs={{0,32},{32,0},{64,96},{96,64},{1,33},{33,1},{65,97},{97,65},{2,34}... | collective-permute-start | bytes 2949128 | tf_op jit(solution)/shard_map/ppermute | solution.py:447
  174.2 21.0 %collective-permute-start.17 = (f32[4,34,8,256]{3,2,1,0:T(8,128)S(1)}, f32[4,34,8,256]{3,2,1,0:T(8,128)S(1)}, u32[]{:S(2)}, u32[]{:S(2)}) collective-permute-start(f32[4,34,8,256]{3,2,1,0:T(8,128)S(1)} %slice.103), channel_id=1, source_target_pairs={{0,32},{32,0},{64,96},{96,64},{1,33},{33,1},{65,97},{97,65},{2,34}... | collective-permute-start | bytes 3342344 | tf_op jit(solution)/shard_map/ppermute | solution.py:447
  175.0 8.9 %collective-permute-start.10 = (f32[2,30,4,256]{3,2,1,0:T(4,128)S(1)}, f32[2,30,4,256]{3,2,1,0:T(4,128)S(1)}, u32[]{:S(2)}, u32[]{:S(2)}) collective-permute-start(f32[2,30,4,256]{3,2,1,0:T(4,128)S(1)} %slice.117), channel_id=1, source_target_pairs={{0,64},{64,0},{32,96},{96,32},{1,65},{65,1},{33,97},{97,33},{2,66}... | collective-permute-start | bytes 737288 | tf_op jit(solution)/shard_map/ppermute | solution.py:450
  175.8 21.2 %collective-permute-start.20 = (f32[2,34,4,256]{3,2,1,0:T(4,128)S(1)}, f32[2,34,4,256]{3,2,1,0:T(4,128)S(1)}, u32[]{:S(2)}, u32[]{:S(2)}) collective-permute-start(f32[2,34,4,256]{3,2,1,0:T(4,128)S(1)} %slice.127), channel_id=1, source_target_pairs={{0,64},{64,0},{32,96},{96,32},{1,65},{65,1},{33,97},{97,33},{2,66}... | collective-permute-start | bytes 835592 | tf_op jit(solution)/shard_map/ppermute | solution.py:450
  184.0 15.1 %collective-permute-start.11 = (f32[2,30,2,256]{3,2,1,0:T(2,128)S(1)}, f32[2,30,2,256]{3,2,1,0:T(2,128)S(1)}, u32[]{:S(2)}, u32[]{:S(2)}) collective-permute-start(f32[2,30,2,256]{3,2,1,0:T(2,128)S(1)} %get-tuple-element.45), channel_id=1, source_target_pairs={{0,1},{1,2},{2,3},{3,4},{4,5},{5,6},{6,7},{7,8},{8,9},{9,10},{10,1... | collective-permute-start | bytes 368648 | tf_op jit(solution)/shard_map/ppermute | solution.py:318
  186.0 21.6 %collective-permute-start.12 = (f32[2,30,2,256]{3,2,1,0:T(2,128)S(1)}, f32[2,30,2,256]{3,2,1,0:T(2,128)S(1)}, u32[]{:S(2)}, u32[]{:S(2)}) collective-permute-start(f32[2,30,2,256]{3,2,1,0:T(2,128)S(1)} %get-tuple-element.46), channel_id=1, source_target_pairs={{1,0},{2,1},{3,2},{4,3},{5,4},{6,5},{7,6},{8,7},{9,8},{10,9},{11,1... | collective-permute-start | bytes 368648 | tf_op jit(solution)/shard_map/ppermute | solution.py:317
  194.6 17.8 %collective-permute-start.8 = (f32[2,30,8,256]{3,2,1,0:T(8,128)S(1)}, f32[2,30,8,256]{3,2,1,0:T(8,128)S(1)}, u32[]{:S(2)}, u32[]{:S(2)}) collective-permute-start(f32[2,30,8,256]{3,2,1,0:T(8,128)S(1)} %slice.115), channel_id=1, source_target_pairs={{0,64},{64,0},{32,96},{96,32},{1,65},{65,1},{33,97},{97,33},{2,66}... | collective-permute-start | bytes 1474568 | tf_op jit(solution)/shard_map/ppermute | solution.py:449
  195.4 27.1 %collective-permute-start.18 = (f32[2,34,8,256]{3,2,1,0:T(8,128)S(1)}, f32[2,34,8,256]{3,2,1,0:T(8,128)S(1)}, u32[]{:S(2)}, u32[]{:S(2)}) collective-permute-start(f32[2,34,8,256]{3,2,1,0:T(8,128)S(1)} %slice.125), channel_id=1, source_target_pairs={{0,64},{64,0},{32,96},{96,32},{1,65},{65,1},{33,97},{97,33},{2,66}... | collective-permute-start | bytes 1671176 | tf_op jit(solution)/shard_map/ppermute | solution.py:449
  197.2 15.4 %collective-permute-start.21 = (f32[2,34,2,256]{3,2,1,0:T(2,128)S(1)}, f32[2,34,2,256]{3,2,1,0:T(2,128)S(1)}, u32[]{:S(2)}, u32[]{:S(2)}) collective-permute-start(f32[2,34,2,256]{3,2,1,0:T(2,128)S(1)} %get-tuple-element.43), channel_id=1, source_target_pairs={{0,1},{1,2},{2,3},{3,4},{4,5},{5,6},{6,7},{7,8},{8,9},{9,10},{10,1... | collective-permute-start | bytes 417800 | tf_op jit(solution)/shard_map/ppermute | solution.py:318
  199.1 13.5 %collective-permute-start.22 = (f32[2,34,2,256]{3,2,1,0:T(2,128)S(1)}, f32[2,34,2,256]{3,2,1,0:T(2,128)S(1)}, u32[]{:S(2)}, u32[]{:S(2)}) collective-permute-start(f32[2,34,2,256]{3,2,1,0:T(2,128)S(1)} %get-tuple-element.44), channel_id=1, source_target_pairs={{1,0},{2,1},{3,2},{4,3},{5,4},{6,5},{7,6},{8,7},{9,8},{10,9},{11,1... | collective-permute-start | bytes 417800 | tf_op jit(solution)/shard_map/ppermute | solution.py:317

commit v2 on v0

v2 whole, which is shorter than its diff:
```python
import functools

import jax
import jax.numpy as jnp
import numpy as np
from jax import lax
from jax.experimental import pallas as pl
from jax.experimental.pallas import tpu as pltpu
from jax.sharding import PartitionSpec as P

SCALE = 1.0 / (6.0 * 8192.0)
SX = 64
ROWS = 8
NZ = 256
HALF = 128
SUBS = 8
GROUPS = 8
CUTS = (24, 48)
VMEM = 12 * 1024 * 1024
STREAMING = 40 * 1024 * 1024
UNROLL = 4
STRIDE = 16
PLUS = {-2: 1.0, -1: -6.0, 0: 3.0, 1: 2.0}
MINUS = {-1: -2.0, 0: -3.0, 1: 6.0, 2: -1.0}


def padded(n):
    return (n + 7) // 8 * 8


def stencil(taps):
    matrix = np.zeros((NZ, NZ), np.float32)
    for shift, weight in taps.items():
        matrix += weight * np.eye(NZ, k=shift, dtype=np.float32)
    return matrix


def half(h):
    return slice(h * HALF, (h + 1) * HALF)


def eights(start):
    return pl.ds(start if isinstance(start, int) else pl.multiple_of(start, ROWS), ROWS)


def loop(count, body, step=UNROLL, first=0):
    for k in range(first):
        body(k)
    whole = (count - first) // step

    def several(block, carry):
        for k in range(step):
            body(first + block * step + k)
        return carry

    if whole > 0:
        lax.fori_loop(0, whole, several, 0)
    for k in range(first + whole * step, count):
        body(k)


class Padded:
    def __init__(self, ref, low):
        self.ref, self.low = ref, low

    def start(self, x):
        return (x - self.low) * STRIDE + ROWS

    def read(self, h, x, shift=0):
        start = self.start(x)
        return self.ref[h, eights(start) if shift == 0 else pl.ds(start + shift, ROWS), :]

    def write(self, h, x, value):
        self.ref[h, eights(self.start(x)), :] = value

    def every(self, x, row):
        return pl.ds(self.start(x) + row, ROWS, stride=STRIDE)


def pad_rows(slices):
    return (2, slices * STRIDE + 2 * ROWS, HALF)


def upwind(speed, back2, back1, mid3, fore1, fore2):
    speed = speed.astype(jnp.float32)
    forward = speed > 0.0
    near = jnp.where(forward, back1, fore1)
    far = jnp.where(forward, back2, fore2)
    ahead = jnp.where(forward, fore1, back1)
    return jnp.abs(speed) * (far - 6.0 * near + mid3 + (ahead + ahead))


def split(value):
    high = value.astype(jnp.bfloat16)
    return high, (value - high.astype(jnp.float32)).astype(jnp.bfloat16)


def fill(field, ref):
    def body(x):
        for h in range(2):
            field.write(h, x, ref[0, x, :, half(h)])

    loop(SX, body)


def clear(ref):
    ref[...] = jnp.zeros_like(ref)


def every(x, row):
    return pl.ds(x * ROWS + row, ROWS, stride=ROWS)


def of(x):
    return eights(x * ROWS)


def put_rows(dst, top, bottom, low, high, base):
    for x in range(low, high, ROWS):
        for h in range(2):
            for r in range(2):
                dst[h, every(x - base, r), :] = top[0, r, x:x + ROWS, half(h)]
                dst[h, every(x - base, 6 + r), :] = bottom[0, r, x:x + ROWS, half(h)]


def advance(field, velocity, weights, lhs, along, emit):
    def halves(k):
        x = k * 2
        for h in range(2):
            pair = jnp.concatenate([field.read(h, x), field.read(h, x + 1)], axis=0)
            high, rest = split(pair)
            rows = pl.ds(k * 16 if isinstance(k, int) else pl.multiple_of(k * 16, 16), 16)
            lhs[rows, half(h)] = high
            lhs[rows, half(2 + h)] = rest

    loop(SX // 2, halves, UNROLL // 2)
    along[...] = jnp.dot(lhs[...], weights[...], preferred_element_type=jnp.float32)

    def body(x):
        for h in range(2):
            mid = field.read(h, x)
            mid3 = 3.0 * mid
            speed = [velocity[0, d, x, :, half(h)] for d in range(3)]
            change = upwind(speed[0], *(field.read(h, x + s) if s else mid3 for s in (-2, -1, 0, 1, 2)))
            change += upwind(speed[1], *(field.read(h, x, s) if s else mid3 for s in (-2, -1, 0, 1, 2)))
            ahead = speed[2].astype(jnp.float32)
            plus, minus = along[of(x), half(h)], along[of(x), half(2 + h)]
            change += ahead * jnp.where(ahead > 0.0, plus, minus)
            emit(h, x, mid - SCALE * change, speed)

    loop(SX, body)


def first_kernel(s, groups, template, weights, moved, sides, pad, speeds, lhs, along, velocity):
    @pl.when(s == 0)
    def start():
        clear(pad)

    field = Padded(pad, -2)
    fill(field, template)

    def emit(h, x, value, speed):
        moved[0, h, of(x), :] = value
        speeds[h, of(x), :] = speed[1].astype(jnp.float32)

    advance(field, velocity, weights, lhs, along, emit)
    for x in range(0, SX, ROWS):
        for h in range(2):
            for i, r in enumerate((0, 1, 6, 7)):
                sides[0, i, x:x + ROWS, half(h)] = speeds[h, every(x, r), :]


def entering(value, speed, prev, next_, k, h):
    group = slice(k, k + ROWS)
    back2, back1 = prev[0, 0, group, half(h)], prev[0, 1, group, half(h)]
    fore1, fore2 = next_[0, 0, group, half(h)], next_[0, 1, group, half(h)]
    v0, v1, v6, v7 = (speed[0, i, group, half(h)] for i in range(4))
    change = (
        jnp.abs(v0) * jnp.where(v0 > 0.0, back2 - 6.0 * back1, 2.0 * back1),
        jnp.maximum(v1, 0.0) * back1,
        jnp.maximum(-v6, 0.0) * fore1,
        jnp.abs(v7) * jnp.where(v7 > 0.0, 2.0 * fore1, fore2 - 6.0 * fore1),
    )
    return [value[0, h, every(k, r), :] - SCALE * c for r, c in zip((0, 1, 6, 7), change)]


class Picked:
    def __init__(self, yes, first, second):
        self.yes, self.first, self.second = yes, first, second

    def __getitem__(self, index):
        return jnp.where(self.yes, self.first[index], self.second[index])


def arrivals(side, even, odd):
    yes = side[2] == 1
    return Picked(yes, even, odd), Picked(yes, odd, even)


def departures(side, both):
    return both.at[1 - side[2]], both.at[side[2]]


def first_border(s, groups, side, moved, even_own, even_other, odd_own, odd_other, sides, both):
    own = (groups[s] // (GROUPS // 2)) == side[0]
    up, down = departures(side, both)

    def finish(even, odd):
        prev, next_ = arrivals(side, even, odd)
        for k in range(0, SX, ROWS):
            for h in range(2):
                rows = entering(moved, sides, prev, next_, k, h)
                for r in range(2):
                    up[0, r, k:k + ROWS, half(h)] = rows[r]
                    down[0, r, k:k + ROWS, half(h)] = rows[2 + r]

    @pl.when(own)
    def from_own():
        finish(even_own, odd_own)

    @pl.when(jnp.logical_not(own))
    def from_other():
        finish(even_other, odd_other)


def second_kernel(s, groups, side, moved, both, images, weights, residual, pad, lhs, along, velocity):
    @pl.when(s == 0)
    def start():
        clear(pad)

    field = Padded(pad, -2)
    up, down = departures(side, both)

    def copy(x):
        for h in range(2):
            field.write(h, x, moved[0, h, of(x), :])

    loop(SX, copy)
    for x in range(0, SX, ROWS):
        for h in range(2):
            for r in range(2):
                pad[h, field.every(x, r), :] = up[0, r, x:x + ROWS, half(h)]
                pad[h, field.every(x, 6 + r), :] = down[0, r, x:x + ROWS, half(h)]

    def emit(h, x, value, speed):
        residual[0, h, of(x), :] = value - images[0, x, :, half(h)]

    advance(field, velocity, weights, lhs, along, emit)


def second_border(s, groups, side, residual, even, odd, sides, top, bottom, both):
    prev, next_ = arrivals(side, even, odd)
    up, down = departures(side, both)
    for k in range(0, SX, ROWS):
        group = slice(k, k + ROWS)
        for h in range(2):
            rows = dict(zip((0, 1, 6, 7), entering(residual, sides, prev, next_, k, h)))
            speed = dict(zip((0, 1, 6, 7), (sides[0, i, group, half(h)] for i in range(4))))
            for r in range(2):
                top[0, r, group, half(h)] = rows[r]
                bottom[0, r, group, half(h)] = rows[6 + r]
            pos = {r: jnp.maximum(speed[r], 0.0) * rows[r] for r in (0, 1, 7)}
            neg = {r: jnp.minimum(speed[r], 0.0) * rows[r] for r in (0, 6, 7)}
            for ref, r, change in outgoing(pos, neg):
                (up, down)[ref][0, r, group, half(h)] = change


def outgoing(pos, neg):
    return (
        (0, 0, -SCALE * pos[0]),
        (0, 1, -SCALE * (pos[1] - 6.0 * pos[0] - 2.0 * neg[0])),
        (1, 0, -SCALE * (2.0 * pos[7] + 6.0 * neg[7] - neg[6])),
        (1, 1, SCALE * neg[7]),
    )


def retreat(low, high, value, base, near, velocity, emit, weights, pos_pad, neg_pad, lhs, along):
    def get(h, x):
        return value[h, of(x - base), :]

    def speed_of(d, h, x):
        return velocity[0, d, x - near, :, half(h)]

    n = high - low
    pos_field, neg_field = Padded(pos_pad, low), Padded(neg_pad, low)

    def before(k):
        x = low + k * 2
        rows = pl.ds(k * 16 if isinstance(k, int) else pl.multiple_of(k * 16, 16), 16)
        for h in range(2):
            pairs = []
            for i in range(2):
                here = get(h, x + i)
                speed = speed_of(1, h, x + i).astype(jnp.float32)
                pos_field.write(h, x + i, jnp.maximum(speed, 0.0) * here)
                neg_field.write(h, x + i, jnp.minimum(speed, 0.0) * here)
                speed = speed_of(2, h, x + i).astype(jnp.float32)
                pairs.append((jnp.maximum(speed, 0.0) * here, jnp.minimum(speed, 0.0) * here))
            for j in range(2):
                top, rest = split(jnp.concatenate([pairs[0][j], pairs[1][j]], axis=0))
                lhs[rows, half(4 * j + h)] = top
                lhs[rows, half(4 * j + 2 + h)] = rest

    loop(n // 2, before, UNROLL // 2)
    along[...] = jnp.dot(lhs[...], weights[...], preferred_element_type=jnp.float32)

    def one(h, x, carry, inside):
        now0, now1, now2, now3 = carry
        here = get(h, x)
        twice = here + here
        speed = speed_of(0, h, x).astype(jnp.float32)
        pos, neg = jnp.maximum(speed, 0.0) * twice, jnp.minimum(speed, 0.0) * twice
        if not isinstance(x, int) or x >= low + 2:
            emit(h, x - 2, get(h, x - 2) - SCALE * (now0 + 0.5 * pos))
        if inside:
            ypos, yneg = pos_field.read(h, x), neg_field.read(h, x)
            own = pos_field.read(h, x, 2) - neg_field.read(h, x, -2)
            own += 2.0 * (pos_field.read(h, x, -1) - neg_field.read(h, x, 1))
            own -= 6.0 * (pos_field.read(h, x, 1) - neg_field.read(h, x, -1))
            own += 3.0 * (ypos - yneg) + 1.5 * (pos - neg)
            own += along[eights((x - low) * ROWS), half(h)]
            now2 = now2 + own
        return now1 - (3.0 * pos + neg), now2, now3 + (pos + 3.0 * neg), -0.5 * neg

    def body(x, carry, inside=True):
        return tuple(one(h, x, carry[h], inside) for h in range(2))

    zero = jnp.zeros((ROWS, HALF), jnp.float32)
    carry = ((zero,) * 4,) * 2
    first, last = low + 2, high
    for x in range(max(low - 2, 0), first):
        carry = body(x, carry, low <= x)
    whole = (last - first) // UNROLL

    def several(block, carry):
        for k in range(UNROLL):
            carry = body(first + block * UNROLL + k, carry)
        return carry

    carry = lax.fori_loop(0, whole, several, carry)
    for x in range(first + whole * UNROLL, last):
        carry = body(x, carry)
    for x in range(last, min(high + 2, SX)):
        carry = body(x, carry, False)
    if high == SX:
        for h in range(2):
            emit(h, SX - 2, get(h, SX - 2) - SCALE * carry[h][0])
            emit(h, SX - 1, get(h, SX - 1) - SCALE * carry[h][1])


def third_kernel(s, groups, residual, top, bottom, weights, adjoint, value, pos_pad, neg_pad, lhs, along, velocity):
    @pl.when(s == 0)
    def start():
        clear(pos_pad)
        clear(neg_pad)

    def copy(x):
        for h in range(2):
            value[h, of(x), :] = residual[0, h, of(x), :]

    loop(SX, copy)
    put_rows(value, top, bottom, 0, SX, 0)

    def emit(h, x, result):
        adjoint[0, h, of(x), :] = result

    retreat(0, SX, value, 0, 0, velocity, emit, weights, pos_pad, neg_pad, lhs, along)


def slot_of(group, side):
    owner = group // 2
    core = (owner % 2 == side[0]).astype(jnp.int32)
    return core * 4 + (owner // 2 == side[1]).astype(jnp.int32) * 2 + group % 2


def third_border(s, groups, side, adjoint, even, odd, sides, edges):
    prev, next_ = arrivals(side, even, odd)
    slot = slot_of(groups[s], side)

    @pl.when(s == 0)
    def start():
        clear(edges)

    for k in range(0, SX, ROWS):
        group = slice(k, k + ROWS)
        for h in range(2):
            value = {r: adjoint[0, h, every(k, r), :] + prev[0, r, group, half(h)] for r in (0, 1)}
            value.update({6 + r: adjoint[0, h, every(k, 6 + r), :] + next_[0, r, group, half(h)] for r in (0, 1)})
            speed = dict(zip((0, 1, 6, 7), (sides[0, i, group, half(h)] for i in range(4))))
            pos = {r: jnp.maximum(speed[r], 0.0) * value[r] for r in (0, 1, 7)}
            neg = {r: jnp.minimum(speed[r], 0.0) * value[r] for r in (0, 6, 7)}
            for ref, r, change in outgoing(pos, neg):
                at = (2 * ref + r) * SX + k
                edges[slot, at:at + ROWS, half(h)] += change


def fourth_kernel(low, high, near, s, groups, side, adjoint, even, odd, weights, sums,
                  value, pos_pad, neg_pad, lhs, along, velocity):
    prev, next_ = arrivals(side, even, odd)
    slot = slot_of(groups[s], side)

    @pl.when(s == 0)
    def start():
        for ref in (sums, pos_pad, neg_pad):
            clear(ref)

    base, stop = max(low - 8, 0), min(high + 8, SX)

    def copy(k):
        for h in range(2):
            value[h, of(k), :] = adjoint[0, h, of(base + k), :]

    loop(stop - base, copy)
    for x in range(base, stop, ROWS):
        for h in range(2):
            for r in range(2):
                value[h, every(x - base, r), :] += prev[0, r, x:x + ROWS, half(h)]
                value[h, every(x - base, 6 + r), :] += next_[0, r, x:x + ROWS, half(h)]

    def emit(h, x, result):
        sums[slot, x - low, :, half(h)] += result

    retreat(low, high, value, base, near, velocity, emit, weights, pos_pad, neg_pad, lhs, along)


def call(body, scalars, ins, outs, arrays, scratch, velocity=None, part=(0, SX), nbytes=40_000_000):
    fixed = len(scalars)
    views = [view for view, _ in ins] + [view for _, view in outs]
    low, high = part
    in_specs = [pl.BlockSpec(memory_space=pltpu.SMEM)] * fixed
    in_specs += [pl.BlockSpec(memory_space=space) for _, space in ins]
    if velocity is not None:
        scratch = scratch + [pltpu.VMEM((2, 3, high - low, ROWS, NZ), jnp.int32), pltpu.SemaphoreType.DMA((2,))]
        in_specs += [pl.BlockSpec(memory_space=pltpu.HBM)]
        arrays = arrays + (velocity,)

    def kernel(*refs):
        refs = list(refs)
        more = {}
        if velocity is not None:
            source = refs.pop(fixed + len(ins))
            buffer, sem = refs[-2:]
            refs = refs[:-2]

            def fetch(s, slot):
                return pltpu.make_async_copy(source.at[s, :, pl.ds(low, high - low)], buffer.at[slot], sem.at[slot])

            fetch(0, 0).start()

        def one(s, carry):
            seen = [view(ref, s, refs[0]) for view, ref in zip(views, refs[fixed:])]
            if velocity is not None:
                slot = s % 2

                @pl.when(s + 1 < SUBS)
                def ahead():
                    fetch(s + 1, 1 - slot).start()

                fetch(s, slot).wait()
                more["velocity"] = buffer.at[pl.ds(slot, 1)]
            body(s, *refs[:fixed], *seen, *refs[fixed + len(views):], **more)
            return carry

        lax.fori_loop(0, SUBS, one, 0)

    return pl.pallas_call(
        kernel,
        in_specs=in_specs,
        out_specs=[pl.BlockSpec(memory_space=pltpu.VMEM)] * len(outs),
        out_shape=[jax.ShapeDtypeStruct(shape.shape, shape.dtype) for shape, _ in outs],
        scratch_shapes=scratch,
        compiler_params=pltpu.CompilerParams(vmem_limit_bytes=VMEM if velocity is None else STREAMING),
        cost_estimate=pl.CostEstimate(flops=nbytes, bytes_accessed=nbytes, transcendentals=0),
    )(*scalars, *arrays)


def everything(ref, s, groups):
    return ref


def subject(ref, s, groups):
    return ref.at[pl.ds(s, 1)]


def pair(ref, s, groups):
    return ref.at[:, pl.ds(s, 1)]


def swap(even, odd, count):
    pairs = [[(i, i + 1) for i in range(first, count - 1, 2)] for first in (0, 1)]
    both_ways = [[(a, b) for a, b in part] + [(b, a) for a, b in part] for part in pairs]
    odd = lax.ppermute(odd, "tile", both_ways[1])
    even = lax.ppermute(even, "tile", both_ways[0])
    return even, odd


def shards(template, images, velocity, groups):
    count = lax.axis_size("tile")
    place = lax.axis_index("subj")
    core, high_y = place % 2, place // 2
    some = GROUPS // 2
    core_pairs = [(0, 1), (1, 0), (2, 3), (3, 2)]
    y_pairs = [(0, 2), (2, 0), (1, 3), (3, 1)]
    is_odd = lax.axis_index("tile") % 2 == 1
    side = jnp.stack([core, high_y, is_odd]).astype(jnp.int32)
    plus, minus = stencil(PLUS), stencil(MINUS)
    onward = np.concatenate([plus.T, minus.T], axis=1)
    onward = jnp.asarray(np.concatenate([onward, onward], axis=0), jnp.bfloat16)
    backward = jnp.asarray(np.concatenate([plus, plus, minus, minus], axis=0), jnp.bfloat16)
    f32, bf16 = jnp.float32, jnp.bfloat16
    vmem = lambda shape, dtype=f32: pltpu.VMEM(shape, dtype)
    shape = jax.ShapeDtypeStruct
    field = shape((SUBS, 2, SX * ROWS, HALF), f32)
    edge = shape((SUBS, 2, SX, NZ), f32)
    edges_both = shape((2, SUBS, 2, SX, NZ), f32)
    one, all_ = (subject, pltpu.VMEM), (everything, pltpu.VMEM)
    rows = SX * ROWS

    mine = lax.dynamic_slice_in_dim(template, core * some, some, axis=0)
    ends = jnp.swapaxes(jnp.concatenate([mine[:, :, 0:2], mine[:, :, 6:8]], axis=2), 1, 2)
    up, down = ends[:, 0:2], ends[:, 2:4]
    even_own, odd_own = swap(jnp.where(is_odd, up, down), jnp.where(is_odd, down, up), count)

    moved, sides = call(
        first_kernel,
        (groups,),
        [(lambda ref, s, g: ref.at[pl.ds(g[s], 1)], pltpu.VMEM), all_],
        [(field, subject), (shape((SUBS, 4, SX, NZ), f32), subject)],
        (template, onward),
        [vmem(pad_rows(SX + 4)), vmem((2, rows, HALF)), vmem((rows, 2 * NZ), bf16), vmem((rows, 2 * NZ))],
        velocity=velocity,
    )
    even_own, odd_own, sides = lax.optimization_barrier((even_own, odd_own, sides))
    even_other = lax.ppermute(even_own, "subj", core_pairs)
    odd_other = lax.ppermute(odd_own, "subj", core_pairs)
    of_group = (lambda ref, s, g: ref.at[pl.ds(g[s] % some, 1)], pltpu.VMEM)
    (both,) = call(
        first_border,
        (groups, side),
        [one] + [of_group] * 4 + [one],
        [(edges_both, pair)],
        (moved, even_own, even_other, odd_own, odd_other, sides),
        [],
    )
    even, odd = swap(both[0], both[1], count)
    (residual,) = call(
        second_kernel,
        (groups, side),
        [one, (pair, pltpu.VMEM), one, all_],
        [(field, subject)],
        (moved, both, images, onward),
        [vmem(pad_rows(SX + 4)), vmem((rows, 2 * NZ), bf16), vmem((rows, 2 * NZ))],
        velocity=velocity,
    )
    top, bottom, both = call(
        second_border,
        (groups, side),
        [one] * 4,
        [(edge, subject)] * 2 + [(edges_both, pair)],
        (residual, even, odd, sides),
        [],
    )
    even, odd = swap(both[0], both[1], count)
    (adjoint,) = call(
        third_kernel,
        (groups,),
        [one] * 3 + [all_],
        [(field, subject)],
        (residual, top, bottom, backward),
        [
            vmem((2, rows, HALF)),
            vmem(pad_rows(SX + 8)),
            vmem(pad_rows(SX + 8)),
            vmem((rows, 4 * NZ), bf16),
            vmem((rows, NZ)),
        ],
        velocity=velocity,
    )

    (edges,) = call(
        third_border,
        (groups, side),
        [one] * 4,
        [(shape((GROUPS, 4 * SX, NZ), f32), everything)],
        (adjoint, even, odd, sides),
        [],
    )
    adjoint, edges = lax.optimization_barrier((adjoint, edges))
    edges4 = edges[some:] + lax.ppermute(edges[:some], "subj", core_pairs)

    cuts = (0,) + CUTS + (SX,)
    sums4, sums2 = [], []
    for c, (low, high) in enumerate(zip(cuts, cuts[1:])):
        n = high - low
        span = min(high + 8, SX) - max(low - 8, 0)
        part = (max(low - 2, 0), min(high + 2, SX))
        if c == 1:
            adjoint, sums4[0] = lax.optimization_barrier((adjoint, sums4[0]))
        if c == 2:
            adjoint, ends, sums2[0] = lax.optimization_barrier((adjoint, ends, sums2[0]))
            ends = ends[2:] + lax.ppermute(ends[:2], "subj", y_pairs)
        (sums,) = call(
            functools.partial(fourth_kernel, low, high, part[0]),
            (groups, side),
            [one] * 3 + [all_],
            [(shape((GROUPS, n, ROWS, NZ), f32), everything)],
            (adjoint, even, odd, backward),
            [
                vmem((2, span * ROWS, HALF)),
                vmem(pad_rows(n + 8)),
                vmem(pad_rows(n + 8)),
                vmem((n * ROWS, 4 * NZ), bf16),
                vmem((n * ROWS, NZ)),
            ],
            velocity=velocity,
            part=part,
        )
        adjoint, sums = lax.optimization_barrier((adjoint, sums))
        if c == 0:
            sums, edges4 = lax.optimization_barrier((sums, edges4))
            up, down = edges4[:, :2 * SX], edges4[:, 2 * SX:]
            ends = swap(jnp.where(is_odd, up, down), jnp.where(is_odd, down, up), count)
        if c == 1:
            sums, *ends = lax.optimization_barrier((sums, *ends))
            ends = jnp.concatenate([jnp.where(is_odd, *ends), jnp.where(is_odd, *ends[::-1])], axis=1)
        if c == 2:
            sums, ends = lax.optimization_barrier((sums, ends))
        sums4.append(sums[some:] + lax.ppermute(sums[:some], "subj", core_pairs))
        sums2.append(sums4[c][2:] + lax.ppermute(sums4[c][:2], "subj", y_pairs))
    from_prev, from_next = ends[:, :2 * SX], ends[:, 2 * SX:]
    middle = jnp.zeros((2, SX, ROWS - 4, NZ), f32)
    from_prev, from_next = (jnp.swapaxes(e.reshape(2, 2, SX, NZ), 1, 2) for e in (from_prev, from_next))
    return jnp.concatenate(sums2, axis=1) + jnp.concatenate([from_prev, middle, from_next], axis=2)


def solution(mesh):
    in_specs = (
        P(None, None, "tile", None),
        P("subj", None, "tile", None),
        P("subj", None, None, "tile", None),
        P("subj"),
    )
    out_specs = P("subj", None, "tile", None)
    return jax.shard_map(shards, mesh=mesh, in_specs=in_specs, out_specs=out_specs, check_vma=False)
```

time: 444 us -> 172 us (0.39)
  other arithmetic: 141 us -> 2.45 us
  waiting for transfers between devices: 160 us -> 56.1 us
  Pallas kernels: 0 us -> 76.4 us
  matrix products: 56 us -> 0 us
  local copies, waits for them, and re-layouts: 29.1 us -> 8.05 us
  starting transfers between devices: 43.5 us -> 27.4 us
  between operations: 13.6 us -> 0.48 us
    mul x4 -> x0, other arithmetic: 106 us -> none  [the longest x2 80.8 us: retreat(): forward_part * adjoint_mid]
    pallas_call x0 -> x9, Pallas kernels: none -> 76.4 us  [call(): pl.pallas_call(kernel, in_specs=in_specs, out_specs=[pl.BlockSpec(memory_...]
    dot_general x2 -> x0, matrix products: 56 us -> none  [the longest x1 49.5 us: shards(): jnp.einsum('sg,sxyz->gxyz', onehot, adjoint, precision=lax.Precision.HIGH...]
    ppermute x8 -> x18, waiting for transfers between devices: 112 us -> 56.1 us  [the longest x3 19.6 us: shards(): sums2.append(sums4[c][2:] + lax.ppermute(sums4[c][:2], 'subj', y_pairs))]
    reduce_scatter x1 -> x0, waiting for transfers between devices: 48.2 us -> none  [shards(): lax.psum_scatter(partial_sums, 'subj', scatter_dimension=0, tiled=True)]
    squeeze x2, local copies, waits for them, and re-layouts: 21.8 us -> 0.4 us  [shards(): even, odd = swap(both[0], both[1], count)]
    ppermute x8 -> x18, starting transfers between devices: 43.5 us -> 27.4 us  [the longest x4 20.2 us: swap(): odd = lax.ppermute(odd, 'tile', both_ways[1])]
    sub x1 -> x0, other arithmetic: 11.5 us -> none  [advance(): result = result - backward_part * stencil_valid(source, along, UPWIND_NEG)]
  transfers between devices with their start and end apart: 9 -> 18, of which waited for: 9 -> 12; matrix products, arithmetic and copies ran while one was open for 4% -> 1% of each run, Pallas kernels for 0% -> 41%
where the time goes in v2:
time: 172 us; the launch traced here: 171 us
  Pallas kernels  76.4 us (44%)
  waiting for transfers between devices  56.1 us (33%)
  starting transfers between devices  27.4 us (16%)
  local copies, waits for them, and re-layouts  8.05 us (5%)
  other arithmetic  2.45 us (1%)
    pallas_call x9, Pallas kernels, call(): pl.pallas_call(kernel, in_specs=in_specs, out_specs=[pl.BlockSpec(memory_...  76.4 us
    ppermute x4, starting transfers between devices, swap(): odd = lax.ppermute(odd, 'tile', both_ways[1])  20.2 us
    ppermute x3, waiting for transfers between devices, shards(): sums2.append(sums4[c][2:] + lax.ppermute(sums4[c][:2], 'subj', y_pairs))  19.6 us
    ppermute x4, waiting for transfers between devices, swap(): odd = lax.ppermute(odd, 'tile', both_ways[1])  19.1 us
    ppermute x4, waiting for transfers between devices, swap(): even = lax.ppermute(even, 'tile', both_ways[0])  9.25 us
    ppermute x1, waiting for transfers between devices, shards(): ends = ends[2:] + lax.ppermute(ends[:2], 'subj', y_pairs)  4.96 us
    unnamed x16, local copies, waits for them, and re-layouts  4.25 us
  transfers between devices with their start and end apart: 18, of which 12 were waited for; matrix products, arithmetic and copies ran while one was open for 1% of the time, Pallas kernels for 41%

profile of v2, /device:TPU:2, one launch (start us, length us, event | category | flops | bytes accessed | tf_op | source)
XLA Modules:
  0.0 171.0 jit_solution(5726376406414555880)
XLA Ops:
  0.0 2.6 %constant_dynamic-slice_fusion = (f32[4,64,2,256]{3,2,1,0:T(2,128)S(1)}, f32[4,64,2,256]{3,2,1,0:T(2,128)S(1)}) fusion(f32[8,64,8,256]{3,2,1,0:T(8,128)} %refs_1_.1, s32[]{:T(128)S(6)} %select_n.54, s32[]{:T(128)S(6)} %add.52), kind=kLoop, calls=%fused_computation.24 | loop fusion | bytes 2097160 | tf_op jit(solution)/shard_map/slice | solution.py:520
  2.9 2.0 %collective-permute-start = (f32[4,2,64,256]{3,2,1,0:T(8,128)S(1)}, f32[4,2,64,256]{3,2,1,0:T(8,128)S(1)}, u32[]{:S(2)}, u32[]{:S(2)}) collective-permute-start(f32[4,2,64,256]{3,2,1,0:T(8,128)S(1)} %get-tuple-element.68), channel_id=1, source_target_pairs={{0,1},{2,3},{4,5},{6,7},{8,9},{10,11},{12,13},{14,15},{16,17},{18,... | collective-permute-start | bytes 1572872 | tf_op jit(solution)/shard_map/ppermute | solution.py:493
  4.9 7.2 %collective-permute-start.1 = (f32[4,2,64,256]{3,2,1,0:T(8,128)S(1)}, f32[4,2,64,256]{3,2,1,0:T(8,128)}, u32[]{:S(2)}, u32[]{:S(2)}) collective-permute-start(f32[4,2,64,256]{3,2,1,0:T(8,128)S(1)} %get-tuple-element.67), channel_id=1, source_target_pairs={{1,2},{3,4},{5,6},{7,8},{9,10},{11,12},{13,14},{15,16},{17,18},{19... | collective-permute-start | bytes 1572872 | tf_op jit(solution)/shard_map/ppermute | solution.py:492
  12.1 13.7 %shard_map.64 = (f32[8,2,512,128]{3,2,1,0:T(8,128)S(1)}, f32[8,4,64,256]{3,2,1,0:T(8,128)S(1)}) custom-call(s32[8]{0:T(128)S(1)} %copy-done.6, f32[8,64,8,256]{3,2,1,0:T(8,128)S(1)} %copy-done.4, bf16[512,512]{1,0:T(8,128)(2,1)S(1)} %copy-done.5, s32[8,3,64,8,256]{4,3,2,1,0:T(8,128)} %refs_6_.7), custom_call_target="tpu_custom_call" | custom-call | flops 40000000 | bytes 40000000 | tf_op jit(solution)/shard_map/pallas_call | solution.py:466
  25.9 1.9 %copy-done = f32[8,2,512,128]{3,2,1,0:T(8,128)} copy-done((f32[8,2,512,128]{3,2,1,0:T(8,128)}, f32[8,2,512,128]{3,2,1,0:T(8,128)S(1)}, u32[]{:S(2)}) %copy-start) | copy-done | bytes 4194328
  28.4 1.5 collective-permute-done.2.refs_4_
  29.9 1.0 collective-permute-done.3.refs_6_
  30.8 2.2 %copy-done.1 = f32[8,2,512,128]{3,2,1,0:T(8,128)S(1)} copy-done((f32[8,2,512,128]{3,2,1,0:T(8,128)S(1)}, f32[8,2,512,128]{3,2,1,0:T(8,128)}, u32[]{:S(2)}) %copy-start.1) | copy-done | bytes 4194328
  33.0 2.3 %shard_map.65.refs_3_ = f32[2,8,2,64,256]{4,3,2,1,0:T(8,128)S(1)} custom-call(s32[8]{0:T(128)S(1)} %copy-done.6, s32[3]{0:T(128)S(1)} %pad_add_fusion.refs_1_, f32[8,2,512,128]{3,2,1,0:T(8,128)S(1)} %copy-done.1, f32[4,2,64,256]{3,2,1,0:T(8,128)S(1)} %collective-permute-done.refs_3_, f32[4,2,64,256]{3,2,1,0:T(8,128)} %collective-permute-done.2.refs_4_, ...), custom_call_target="tpu_custom_call" | custom-call | flops 40000000 | bytes 40000000 | tf_op jit(solution)/shard_map/pallas_call | solution.py:466
  35.6 4.5 %collective-permute-start.5 = (f32[8,2,64,256]{3,2,1,0:T(8,128)S(1)}, f32[8,2,64,256]{3,2,1,0:T(8,128)S(1)}, u32[]{:S(2)}, u32[]{:S(2)}) collective-permute-start(f32[8,2,64,256]{3,2,1,0:T(8,128)S(1)} %get-tuple-element.61), channel_id=1, source_target_pairs={{1,2},{3,4},{5,6},{7,8},{9,10},{11,12},{13,14},{15,16},{17,18},{19... | collective-permute-start | bytes 3145736 | tf_op jit(solution)/shard_map/ppermute | solution.py:492
  40.2 16.1 %shard_map.66.refs_2_.refs_1_ = f32[8,2,512,128]{3,2,1,0:T(8,128)S(1)} custom-call(s32[8]{0:T(128)S(1)} %copy-done.6, s32[3]{0:T(128)S(1)} %pad_add_fusion.refs_1_, f32[8,2,512,128]{3,2,1,0:T(8,128)S(1)} %copy-done.2, f32[2,8,2,64,256]{4,3,2,1,0:T(8,128)S(1)} %shard_map.65.refs_3_, f32[8,64,8,256]{3,2,1,0:T(8,128)} %refs_4_.2, ...), custom_call_target="tpu_custom_call" | custom-call | flops 40000000 | bytes 40000000 | tf_op jit(solution)/shard_map/pallas_call | solution.py:466
  56.3 4.5 %collective-permute-done.4.refs_3_ = f32[8,2,64,256]{3,2,1,0:T(8,128)S(1)} collective-permute-done((f32[8,2,64,256]{3,2,1,0:T(8,128)S(1)}, f32[8,2,64,256]{3,2,1,0:T(8,128)S(1)}, u32[]{:S(2)}, u32[]{:S(2)}) %collective-permute-start.4) | collective-permute-done | bytes 1048608 | tf_op jit(solution)/shard_map/ppermute | solution.py:493
  60.8 6.7 %collective-permute-done.5.refs_4_ = f32[8,2,64,256]{3,2,1,0:T(8,128)S(1)} collective-permute-done((f32[8,2,64,256]{3,2,1,0:T(8,128)S(1)}, f32[8,2,64,256]{3,2,1,0:T(8,128)S(1)}, u32[]{:S(2)}, u32[]{:S(2)}) %collective-permute-start.5) | collective-permute-done | bytes 1048608 | tf_op jit(solution)/shard_map/ppermute | solution.py:492
  67.5 1.6 shard_map.67
  69.4 4.3 %collective-permute-start.7 = (f32[8,2,64,256]{3,2,1,0:T(8,128)S(1)}, f32[8,2,64,256]{3,2,1,0:T(8,128)S(1)}, u32[]{:S(2)}, u32[]{:S(2)}) collective-permute-start(f32[8,2,64,256]{3,2,1,0:T(8,128)S(1)} %get-tuple-element.59), channel_id=1, source_target_pairs={{1,2},{3,4},{5,6},{7,8},{9,10},{11,12},{13,14},{15,16},{17,18},{19... | collective-permute-start | bytes 3145736 | tf_op jit(solution)/shard_map/ppermute | solution.py:492
  73.7 15.3 %shard_map.68.refs_2_ = f32[8,2,512,128]{3,2,1,0:T(8,128)S(1)} custom-call(s32[8]{0:T(128)S(1)} %copy-done.6, f32[8,2,512,128]{3,2,1,0:T(8,128)S(1)} %shard_map.66.refs_2_.refs_1_, f32[8,2,64,256]{3,2,1,0:T(8,128)S(1)} %get-tuple-element.36.refs_2_, f32[8,2,64,256]{3,2,1,0:T(8,128)S(1)} %get-tuple-element.37.refs_3_, bf16[1024,256]{1,0:T(8,128)(2,1)S(1)} %copy-done.3, ...), custom_call_target="tpu_custom_call" | custom-call | flops 40000000 | bytes 40000000 | tf_op jit(solution)/shard_map/pallas_call | solution.py:466
  89.0 4.8 %collective-permute-done.6.refs_3_ = f32[8,2,64,256]{3,2,1,0:T(8,128)S(1)} collective-permute-done((f32[8,2,64,256]{3,2,1,0:T(8,128)S(1)}, f32[8,2,64,256]{3,2,1,0:T(8,128)S(1)}, u32[]{:S(2)}, u32[]{:S(2)}) %collective-permute-start.6) | collective-permute-done | bytes 1048608 | tf_op jit(solution)/shard_map/ppermute | solution.py:493
  93.8 6.4 %collective-permute-done.7.refs_4_ = f32[8,2,64,256]{3,2,1,0:T(8,128)S(1)} collective-permute-done((f32[8,2,64,256]{3,2,1,0:T(8,128)S(1)}, f32[8,2,64,256]{3,2,1,0:T(8,128)S(1)}, u32[]{:S(2)}, u32[]{:S(2)}) %collective-permute-start.7) | collective-permute-done | bytes 1048608 | tf_op jit(solution)/shard_map/ppermute | solution.py:492
  100.2 1.6 shard_map.69
  102.0 8.9 %shard_map.70 = f32[8,24,8,256]{3,2,1,0:T(8,128)S(1)} custom-call(s32[8]{0:T(128)S(1)} %copy-done.6, s32[3]{0:T(128)S(1)} %pad_add_fusion.refs_1_, f32[8,2,512,128]{3,2,1,0:T(8,128)S(1)} %shard_map.68.refs_2_, f32[8,2,64,256]{3,2,1,0:T(8,128)S(1)} %collective-permute-done.6.refs_3_, f32[8,2,64,256]{3,2,1,0:T(8,128)S(1)} %collective-permute-done.7.refs_4_, ...), custom_call_target="tpu_custom_call" | custom-call | flops 40000000 | bytes 40000000 | tf_op jit(solution)/shard_map/pallas_call | solution.py:466
  111.9 4.3 %collective-permute-start.11 = (f32[4,128,256]{2,1,0:T(8,128)S(1)}, f32[4,128,256]{2,1,0:T(8,128)S(1)}, u32[]{:S(2)}, u32[]{:S(2)}) collective-permute-start(f32[4,128,256]{2,1,0:T(8,128)S(1)} %get-tuple-element.65), channel_id=1, source_target_pairs={{1,2},{3,4},{5,6},{7,8},{9,10},{11,12},{13,14},{15,16},{17,18},{19... | collective-permute-start | bytes 1572872 | tf_op jit(solution)/shard_map/ppermute | solution.py:492
  117.1 9.2 %shard_map.71 = f32[8,24,8,256]{3,2,1,0:T(8,128)S(1)} custom-call(s32[8]{0:T(128)S(1)} %copy-done.6, s32[3]{0:T(128)S(1)} %pad_add_fusion.refs_1_, f32[8,2,512,128]{3,2,1,0:T(8,128)S(1)} %shard_map.68.refs_2_, f32[8,2,64,256]{3,2,1,0:T(8,128)S(1)} %collective-permute-done.6.refs_3_, f32[8,2,64,256]{3,2,1,0:T(8,128)S(1)} %collective-permute-done.7.refs_4_, ...), custom_call_target="tpu_custom_call" | custom-call | flops 40000000 | bytes 40000000 | tf_op jit(solution)/shard_map/pallas_call | solution.py:466
  126.3 6.0 %collective-permute-done.11 = f32[4,128,256]{2,1,0:T(8,128)S(1)} collective-permute-done((f32[4,128,256]{2,1,0:T(8,128)S(1)}, f32[4,128,256]{2,1,0:T(8,128)S(1)}, u32[]{:S(2)}, u32[]{:S(2)}) %collective-permute-start.11) | collective-permute-done | bytes 524320 | tf_op jit(solution)/shard_map/ppermute | solution.py:492
  132.5 5.6 %collective-permute-done.12 = f32[2,24,8,256]{3,2,1,0:T(8,128)S(1)} collective-permute-done((f32[2,24,8,256]{3,2,1,0:T(8,128)S(1)}, f32[2,24,8,256]{3,2,1,0:T(8,128)S(1)}, u32[]{:S(2)}, u32[]{:S(2)}) %collective-permute-start.12) | collective-permute-done | bytes 393248 | tf_op jit(solution)/shard_map/ppermute | solution.py:629
  138.2 1.2 collective-permute-start.15
  139.5 7.6 %shard_map.72 = f32[8,16,8,256]{3,2,1,0:T(8,128)S(1)} custom-call(s32[8]{0:T(128)S(1)} %copy-done.6, s32[3]{0:T(128)S(1)} %pad_add_fusion.refs_1_, f32[8,2,512,128]{3,2,1,0:T(8,128)S(1)} %shard_map.68.refs_2_, f32[8,2,64,256]{3,2,1,0:T(8,128)S(1)} %collective-permute-done.6.refs_3_, f32[8,2,64,256]{3,2,1,0:T(8,128)S(1)} %collective-permute-done.7.refs_4_, ...), custom_call_target="tpu_custom_call" | custom-call | flops 40000000 | bytes 40000000 | tf_op jit(solution)/shard_map/pallas_call | solution.py:466
  147.1 5.0 %collective-permute-done.15 = f32[2,256,256]{2,1,0:T(8,128)S(1)} collective-permute-done((f32[2,256,256]{2,1,0:T(8,128)S(1)}, f32[2,256,256]{2,1,0:T(8,128)S(1)}, u32[]{:S(2)}, u32[]{:S(2)}) %collective-permute-start.15) | collective-permute-done | bytes 524320 | tf_op jit(solution)/shard_map/ppermute | solution.py:601
  152.4 0.8 collective-permute-start.14
  153.3 0.9 collective-permute-done.16
  155.6 8.9 %collective-permute-done.14 = f32[2,24,8,256]{3,2,1,0:T(8,128)S(1)} collective-permute-done((f32[2,24,8,256]{3,2,1,0:T(8,128)S(1)}, f32[2,24,8,256]{3,2,1,0:T(8,128)S(1)}, u32[]{:S(2)}, u32[]{:S(2)}) %collective-permute-start.14) | collective-permute-done | bytes 393248 | tf_op jit(solution)/shard_map/ppermute | solution.py:629
  164.5 5.2 %collective-permute-done.17 = f32[2,16,8,256]{3,2,1,0:T(8,128)S(1)} collective-permute-done((f32[2,16,8,256]{3,2,1,0:T(8,128)S(1)}, f32[2,16,8,256]{3,2,1,0:T(8,128)S(1)}, u32[]{:S(2)}, u32[]{:S(2)}) %collective-permute-start.17) | collective-permute-done | bytes 262176 | tf_op jit(solution)/shard_map/ppermute | solution.py:629
  169.7 1.3 maximum_add_fusion
  (59 shorter events, 5.8 us)
Async XLA Ops:
  2.6 9.5 %copy-start.5 = (bf16[512,512]{1,0:T(8,128)(2,1)S(1)}, bf16[512,512]{1,0:T(8,128)(2,1)}, u32[]{:S(2)}) copy-start(bf16[512,512]{1,0:T(8,128)(2,1)} %constant.49.clone.refs_2_.refs_5_) | copy-start | bytes 1572868
  2.7 9.4 %copy-start.4 = (f32[8,64,8,256]{3,2,1,0:T(8,128)S(1)}, f32[8,64,8,256]{3,2,1,0:T(8,128)}, u32[]{:S(2)}) copy-start(f32[8,64,8,256]{3,2,1,0:T(8,128)} %refs_1_.1) | copy-start | bytes 12582916
  2.7 9.4 %copy-start.6 = (s32[8]{0:T(128)S(1)}, s32[8]{0:T(128)}, u32[]{:S(2)}) copy-start(s32[8]{0:T(128)} %refs_0_.17) | copy-start | bytes 100
  2.9 24.9 %collective-permute-start = (f32[4,2,64,256]{3,2,1,0:T(8,128)S(1)}, f32[4,2,64,256]{3,2,1,0:T(8,128)S(1)}, u32[]{:S(2)}, u32[]{:S(2)}) collective-permute-start(f32[4,2,64,256]{3,2,1,0:T(8,128)S(1)} %get-tuple-element.68), channel_id=1, source_target_pairs={{0,1},{2,3},{4,5},{6,7},{8,9},{10,11},{12,13},{14,15},{16,17},{18,... | collective-permute-start | bytes 1572872 | tf_op jit(solution)/shard_map/ppermute | solution.py:493
  4.9 22.9 %collective-permute-start.1 = (f32[4,2,64,256]{3,2,1,0:T(8,128)S(1)}, f32[4,2,64,256]{3,2,1,0:T(8,128)}, u32[]{:S(2)}, u32[]{:S(2)}) collective-permute-start(f32[4,2,64,256]{3,2,1,0:T(8,128)S(1)} %get-tuple-element.67), channel_id=1, source_target_pairs={{1,2},{3,4},{5,6},{7,8},{9,10},{11,12},{13,14},{15,16},{17,18},{19... | collective-permute-start | bytes 1572872 | tf_op jit(solution)/shard_map/ppermute | solution.py:492
  25.8 2.0 %copy-start = (f32[8,2,512,128]{3,2,1,0:T(8,128)}, f32[8,2,512,128]{3,2,1,0:T(8,128)S(1)}, u32[]{:S(2)}) copy-start(f32[8,2,512,128]{3,2,1,0:T(8,128)S(1)} %get-tuple-element.31.refs_2_) | copy-start | bytes 12582916
  27.8 2.0 %collective-permute-start.2 = (f32[4,2,64,256]{3,2,1,0:T(8,128)S(1)}, f32[4,2,64,256]{3,2,1,0:T(8,128)}, u32[]{:S(2)}, u32[]{:S(2)}) collective-permute-start(f32[4,2,64,256]{3,2,1,0:T(8,128)S(1)} %collective-permute-done.refs_3_), channel_id=1, source_target_pairs={{0,32},{32,0},{64,96},{96,64},{1,33},{33,1},{65,97},{97,65},{2,34}... | collective-permute-start | bytes 1572872 | tf_op jit(solution)/shard_map/ppermute | solution.py:534
  27.8 3.0 %collective-permute-start.3 = (f32[4,2,64,256]{3,2,1,0:T(8,128)}, f32[4,2,64,256]{3,2,1,0:T(8,128)}, u32[]{:S(2)}, u32[]{:S(2)}) collective-permute-start(f32[4,2,64,256]{3,2,1,0:T(8,128)} %collective-permute-done.1.refs_5_), channel_id=1, source_target_pairs={{0,32},{32,0},{64,96},{96,64},{1,33},{33,1},{65,97},{97,65},{2,34}... | collective-permute-start | bytes 1572872 | tf_op jit(solution)/shard_map/ppermute | solution.py:535
  30.8 2.2 %copy-start.1 = (f32[8,2,512,128]{3,2,1,0:T(8,128)S(1)}, f32[8,2,512,128]{3,2,1,0:T(8,128)}, u32[]{:S(2)}) copy-start(f32[8,2,512,128]{3,2,1,0:T(8,128)} %copy-done) | copy-start | bytes 12582916
  35.3 4.9 %copy-start.2 = (f32[8,2,512,128]{3,2,1,0:T(8,128)S(1)}, f32[8,2,512,128]{3,2,1,0:T(8,128)}, u32[]{:S(2)}) copy-start(f32[8,2,512,128]{3,2,1,0:T(8,128)} %copy-done) | copy-start | bytes 12582916
  35.5 25.3 %collective-permute-start.4 = (f32[8,2,64,256]{3,2,1,0:T(8,128)S(1)}, f32[8,2,64,256]{3,2,1,0:T(8,128)S(1)}, u32[]{:S(2)}, u32[]{:S(2)}) collective-permute-start(f32[8,2,64,256]{3,2,1,0:T(8,128)S(1)} %get-tuple-element.62), channel_id=1, source_target_pairs={{0,1},{2,3},{4,5},{6,7},{8,9},{10,11},{12,13},{14,15},{16,17},{18,... | collective-permute-start | bytes 3145736 | tf_op jit(solution)/shard_map/ppermute | solution.py:493
  35.6 31.9 %collective-permute-start.5 = (f32[8,2,64,256]{3,2,1,0:T(8,128)S(1)}, f32[8,2,64,256]{3,2,1,0:T(8,128)S(1)}, u32[]{:S(2)}, u32[]{:S(2)}) collective-permute-start(f32[8,2,64,256]{3,2,1,0:T(8,128)S(1)} %get-tuple-element.61), channel_id=1, source_target_pairs={{1,2},{3,4},{5,6},{7,8},{9,10},{11,12},{13,14},{15,16},{17,18},{19... | collective-permute-start | bytes 3145736 | tf_op jit(solution)/shard_map/ppermute | solution.py:492
  69.1 4.6 %copy-start.3 = (bf16[1024,256]{1,0:T(8,128)(2,1)S(1)}, bf16[1024,256]{1,0:T(8,128)(2,1)}, u32[]{:S(2)}) copy-start(bf16[1024,256]{1,0:T(8,128)(2,1)} %constant.50.clone.refs_4_.refs_5_) | copy-start | bytes 1572868
  69.3 24.5 %collective-permute-start.6 = (f32[8,2,64,256]{3,2,1,0:T(8,128)S(1)}, f32[8,2,64,256]{3,2,1,0:T(8,128)S(1)}, u32[]{:S(2)}, u32[]{:S(2)}) collective-permute-start(f32[8,2,64,256]{3,2,1,0:T(8,128)S(1)} %get-tuple-element.60), channel_id=1, source_target_pairs={{0,1},{2,3},{4,5},{6,7},{8,9},{10,11},{12,13},{14,15},{16,17},{18,... | collective-permute-start | bytes 3145736 | tf_op jit(solution)/shard_map/ppermute | solution.py:493
  69.4 30.8 %collective-permute-start.7 = (f32[8,2,64,256]{3,2,1,0:T(8,128)S(1)}, f32[8,2,64,256]{3,2,1,0:T(8,128)S(1)}, u32[]{:S(2)}, u32[]{:S(2)}) collective-permute-start(f32[8,2,64,256]{3,2,1,0:T(8,128)S(1)} %get-tuple-element.59), channel_id=1, source_target_pairs={{1,2},{3,4},{5,6},{7,8},{9,10},{11,12},{13,14},{15,16},{17,18},{19... | collective-permute-start | bytes 3145736 | tf_op jit(solution)/shard_map/ppermute | solution.py:492
  101.9 9.0 %collective-permute-start.8 = (f32[4,256,256]{2,1,0:T(8,128)S(1)}, f32[4,256,256]{2,1,0:T(8,128)S(1)}, u32[]{:S(2)}, u32[]{:S(2)}) collective-permute-start(f32[4,256,256]{2,1,0:T(8,128)S(1)} %slice.93), channel_id=1, source_target_pairs={{0,32},{32,0},{64,96},{96,64},{1,33},{33,1},{65,97},{97,65},{2,34}... | collective-permute-start | bytes 3145736 | tf_op jit(solution)/shard_map/ppermute | solution.py:589
  111.2 5.1 %collective-permute-start.9 = (f32[4,24,8,256]{3,2,1,0:T(8,128)S(1)}, f32[4,24,8,256]{3,2,1,0:T(8,128)S(1)}, u32[]{:S(2)}, u32[]{:S(2)}) collective-permute-start(f32[4,24,8,256]{3,2,1,0:T(8,128)S(1)} %slice.95), channel_id=1, source_target_pairs={{0,32},{32,0},{64,96},{96,64},{1,33},{33,1},{65,97},{97,65},{2,34}... | collective-permute-start | bytes 2359304 | tf_op jit(solution)/shard_map/ppermute | solution.py:628
  111.9 14.5 %collective-permute-start.10 = (f32[4,128,256]{2,1,0:T(8,128)S(1)}, f32[4,128,256]{2,1,0:T(8,128)S(1)}, u32[]{:S(2)}, u32[]{:S(2)}) collective-permute-start(f32[4,128,256]{2,1,0:T(8,128)S(1)} %get-tuple-element.66), channel_id=1, source_target_pairs={{0,1},{2,3},{4,5},{6,7},{8,9},{10,11},{12,13},{14,15},{16,17},{18,... | collective-permute-start | bytes 1572872 | tf_op jit(solution)/shard_map/ppermute | solution.py:493
  111.9 20.4 %collective-permute-start.11 = (f32[4,128,256]{2,1,0:T(8,128)S(1)}, f32[4,128,256]{2,1,0:T(8,128)S(1)}, u32[]{:S(2)}, u32[]{:S(2)}) collective-permute-start(f32[4,128,256]{2,1,0:T(8,128)S(1)} %get-tuple-element.65), channel_id=1, source_target_pairs={{1,2},{3,4},{5,6},{7,8},{9,10},{11,12},{13,14},{15,16},{17,18},{19... | collective-permute-start | bytes 1572872 | tf_op jit(solution)/shard_map/ppermute | solution.py:492
  116.4 21.7 %collective-permute-start.12 = (f32[2,24,8,256]{3,2,1,0:T(8,128)S(1)}, f32[2,24,8,256]{3,2,1,0:T(8,128)S(1)}, u32[]{:S(2)}, u32[]{:S(2)}) collective-permute-start(f32[2,24,8,256]{3,2,1,0:T(8,128)S(1)} %slice.117), channel_id=1, source_target_pairs={{0,64},{64,0},{32,96},{96,32},{1,65},{65,1},{33,97},{97,33},{2,66}... | collective-permute-start | bytes 1179656 | tf_op jit(solution)/shard_map/ppermute | solution.py:629
  138.2 13.9 %collective-permute-start.15 = (f32[2,256,256]{2,1,0:T(8,128)S(1)}, f32[2,256,256]{2,1,0:T(8,128)S(1)}, u32[]{:S(2)}, u32[]{:S(2)}) collective-permute-start(f32[2,256,256]{2,1,0:T(8,128)S(1)} %slice.105), channel_id=1, source_target_pairs={{0,64},{64,0},{32,96},{96,32},{1,65},{65,1},{33,97},{97,33},{2,66}... | collective-permute-start | bytes 1572872 | tf_op jit(solution)/shard_map/ppermute | solution.py:601
  139.4 12.9 %collective-permute-start.13 = (f32[4,24,8,256]{3,2,1,0:T(8,128)S(1)}, f32[4,24,8,256]{3,2,1,0:T(8,128)S(1)}, u32[]{:S(2)}, u32[]{:S(2)}) collective-permute-start(f32[4,24,8,256]{3,2,1,0:T(8,128)S(1)} %slice.101), channel_id=1, source_target_pairs={{0,32},{32,0},{64,96},{96,64},{1,33},{33,1},{65,97},{97,65},{2,34}... | collective-permute-start | bytes 2359304 | tf_op jit(solution)/shard_map/ppermute | solution.py:628
  152.2 2.0 %collective-permute-start.16 = (f32[4,16,8,256]{3,2,1,0:T(8,128)S(1)}, f32[4,16,8,256]{3,2,1,0:T(8,128)S(1)}, u32[]{:S(2)}, u32[]{:S(2)}) collective-permute-start(f32[4,16,8,256]{3,2,1,0:T(8,128)S(1)} %slice.107), channel_id=1, source_target_pairs={{0,32},{32,0},{64,96},{96,64},{1,33},{33,1},{65,97},{97,65},{2,34}... | collective-permute-start | bytes 1572872 | tf_op jit(solution)/shard_map/ppermute | solution.py:628
  152.4 12.0 %collective-permute-start.14 = (f32[2,24,8,256]{3,2,1,0:T(8,128)S(1)}, f32[2,24,8,256]{3,2,1,0:T(8,128)S(1)}, u32[]{:S(2)}, u32[]{:S(2)}) collective-permute-start(f32[2,24,8,256]{3,2,1,0:T(8,128)S(1)} %slice.119), channel_id=1, source_target_pairs={{0,64},{64,0},{32,96},{96,32},{1,65},{65,1},{33,97},{97,33},{2,66}... | collective-permute-start | bytes 1179656 | tf_op jit(solution)/shard_map/ppermute | solution.py:629
  154.3 15.3 %collective-permute-start.17 = (f32[2,16,8,256]{3,2,1,0:T(8,128)S(1)}, f32[2,16,8,256]{3,2,1,0:T(8,128)S(1)}, u32[]{:S(2)}, u32[]{:S(2)}) collective-permute-start(f32[2,16,8,256]{3,2,1,0:T(8,128)S(1)} %slice.121), channel_id=1, source_target_pairs={{0,64},{64,0},{32,96},{96,32},{1,65},{65,1},{33,97},{97,33},{2,66}... | collective-permute-start | bytes 786440 | tf_op jit(solution)/shard_map/ppermute | solution.py:629

commit v3 on v2

--- a/solution.py
+++ b/solution.py
@@ -15,8 +15,7 @@
 HALF = 128
 SUBS = 8
 GROUPS = 8
-CUTS = (24, 48)
-VMEM = 12 * 1024 * 1024
+VMEM = 2 * 1024 * 1024
 STREAMING = 40 * 1024 * 1024
 UNROLL = 4
 STRIDE = 16
@@ -585,52 +584,33 @@
         (adjoint, even, odd, sides),
         [],
     )
-    adjoint, edges = lax.optimization_barrier((adjoint, edges))
     edges4 = edges[some:] + lax.ppermute(edges[:some], "subj", core_pairs)
-
-    cuts = (0,) + CUTS + (SX,)
-    sums4, sums2 = [], []
-    for c, (low, high) in enumerate(zip(cuts, cuts[1:])):
-        n = high - low
-        span = min(high + 8, SX) - max(low - 8, 0)
-        part = (max(low - 2, 0), min(high + 2, SX))
-        if c == 1:
-            adjoint, sums4[0] = lax.optimization_barrier((adjoint, sums4[0]))
-        if c == 2:
-            adjoint, ends, sums2[0] = lax.optimization_barrier((adjoint, ends, sums2[0]))
-            ends = ends[2:] + lax.ppermute(ends[:2], "subj", y_pairs)
-        (sums,) = call(
-            functools.partial(fourth_kernel, low, high, part[0]),
-            (groups, side),
-            [one] * 3 + [all_],
-            [(shape((GROUPS, n, ROWS, NZ), f32), everything)],
-            (adjoint, even, odd, backward),
-            [
-                vmem((2, span * ROWS, HALF)),
-                vmem(pad_rows(n + 8)),
-                vmem(pad_rows(n + 8)),
-                vmem((n * ROWS, 4 * NZ), bf16),
-                vmem((n * ROWS, NZ)),
-            ],
-            velocity=velocity,
-            part=part,
-        )
-        adjoint, sums = lax.optimization_barrier((adjoint, sums))
-        if c == 0:
-            sums, edges4 = lax.optimization_barrier((sums, edges4))
-            up, down = edges4[:, :2 * SX], edges4[:, 2 * SX:]
-            ends = swap(jnp.where(is_odd, up, down), jnp.where(is_odd, down, up), count)
-        if c == 1:
-            sums, *ends = lax.optimization_barrier((sums, *ends))
-            ends = jnp.concatenate([jnp.where(is_odd, *ends), jnp.where(is_odd, *ends[::-1])], axis=1)
-        if c == 2:
-            sums, ends = lax.optimization_barrier((sums, ends))
-        sums4.append(sums[some:] + lax.ppermute(sums[:some], "subj", core_pairs))
-        sums2.append(sums4[c][2:] + lax.ppermute(sums4[c][:2], "subj", y_pairs))
-    from_prev, from_next = ends[:, :2 * SX], ends[:, 2 * SX:]
-    middle = jnp.zeros((2, SX, ROWS - 4, NZ), f32)
-    from_prev, from_next = (jnp.swapaxes(e.reshape(2, 2, SX, NZ), 1, 2) for e in (from_prev, from_next))
-    return jnp.concatenate(sums2, axis=1) + jnp.concatenate([from_prev, middle, from_next], axis=2)
+    adjoint, edges4 = lax.optimization_barrier((adjoint, edges4))
+    up, down = edges4[:, :2 * SX], edges4[:, 2 * SX:]
+    even_ends, odd_ends = swap(jnp.where(is_odd, up, down), jnp.where(is_odd, down, up), count)
+    (sums,) = call(
+        functools.partial(fourth_kernel, 0, SX, 0),
+        (groups, side),
+        [one] * 3 + [all_],
+        [(shape((GROUPS, SX, ROWS, NZ), f32), everything)],
+        (adjoint, even, odd, backward),
+        [
+            vmem((2, rows, HALF)),
+            vmem(pad_rows(SX + 8)),
+            vmem(pad_rows(SX + 8)),
+            vmem((rows, 4 * NZ), bf16),
+            vmem((rows, NZ)),
+        ],
+        velocity=velocity,
+    )
+    sums, even_ends, odd_ends = lax.optimization_barrier((sums, even_ends, odd_ends))
+    arrived = lax.ppermute(sums[:some], "subj", core_pairs)
+    middle = jnp.zeros((some, SX, ROWS - 4, NZ), f32)
+    from_prev, from_next = jnp.where(is_odd, even_ends, odd_ends), jnp.where(is_odd, odd_ends, even_ends)
+    from_prev, from_next = (jnp.swapaxes(e.reshape(some, 2, SX, NZ), 1, 2) for e in (from_prev, from_next))
+    sums4 = sums[some:] + jnp.concatenate([from_prev, middle, from_next], axis=2)
+    sums4 = sums4 + arrived
+    return sums4[2:] + lax.ppermute(sums4[:2], "subj", y_pairs)
 
 
 def solution(mesh):

time: 172 us -> 158 us (0.919)
  Pallas kernels: 76.4 us -> 67 us
  starting transfers between devices: 27.4 us -> 24 us
    pallas_call x9 -> x7, Pallas kernels: 76.4 us -> 67 us  [call(): pl.pallas_call(kernel, in_specs=in_specs, out_specs=[pl.BlockSpec(memory_...]
    ppermute x4, waiting for transfers between devices: 19.1 us -> 13.1 us  [swap(): odd = lax.ppermute(odd, 'tile', both_ways[1])]
    ppermute x7 -> x2, starting transfers between devices: 4.35 us -> 0.84 us  [the longest x1 0.75 us: shards(): return sums4[2:] + lax.ppermute(sums4[:2], 'subj', y_pairs)]
    ppermute x1, waiting for transfers between devices: 0.01 us -> 2.65 us  [shards(): edges4 = edges[some:] + lax.ppermute(edges[:some], 'subj', core_pairs)]
    ppermute x7 -> x2, waiting for transfers between devices: 25.4 us -> 27.7 us  [the longest x1 24.5 us: shards(): return sums4[2:] + lax.ppermute(sums4[:2], 'subj', y_pairs)]
  transfers between devices with their start and end apart: 18 -> 13, of which waited for: 12 -> 9; matrix products, arithmetic and copies ran while one was open for 1% -> 1% of each run, Pallas kernels for 41% -> 39%
where the time goes in v3:
time: 158 us; the launch traced here: 157 us
  Pallas kernels  67 us (42%)
  waiting for transfers between devices  55 us (35%)
  starting transfers between devices  24 us (15%)
  local copies, waits for them, and re-layouts  8.38 us (5%)
  other arithmetic  2.4 us (2%)
    pallas_call x7, Pallas kernels, call(): pl.pallas_call(kernel, in_specs=in_specs, out_specs=[pl.BlockSpec(memory_...  67 us
    ppermute x1, waiting for transfers between devices, shards(): return sums4[2:] + lax.ppermute(sums4[:2], 'subj', y_pairs)  24.5 us
    ppermute x4, starting transfers between devices, swap(): odd = lax.ppermute(odd, 'tile', both_ways[1])  20.3 us
    ppermute x4, waiting for transfers between devices, swap(): odd = lax.ppermute(odd, 'tile', both_ways[1])  13.1 us
    ppermute x4, waiting for transfers between devices, swap(): even = lax.ppermute(even, 'tile', both_ways[0])  9.18 us
    unnamed x16, local copies, waits for them, and re-layouts  4.24 us
  transfers between devices with their start and end apart: 13, of which 9 were waited for; matrix products, arithmetic and copies ran while one was open for 1% of the time, Pallas kernels for 39%

profile of v3, /device:TPU:2, one launch (start us, length us, event | category | flops | bytes accessed | tf_op | source)
XLA Modules:
  0.0 157.2 jit_solution(949307386452895791)
XLA Ops:
  0.0 2.6 %constant_dynamic-slice_fusion = (f32[4,64,2,256]{3,2,1,0:T(2,128)S(1)}, f32[4,64,2,256]{3,2,1,0:T(2,128)S(1)}) fusion(f32[8,64,8,256]{3,2,1,0:T(8,128)} %refs_1_.1, s32[]{:T(128)S(6)} %select_n.54, s32[]{:T(128)S(6)} %add.32), kind=kLoop, calls=%fused_computation.18 | loop fusion | bytes 2097160 | tf_op jit(solution)/shard_map/slice | solution.py:519
  2.9 2.0 %collective-permute-start = (f32[4,2,64,256]{3,2,1,0:T(8,128)S(1)}, f32[4,2,64,256]{3,2,1,0:T(8,128)S(1)}, u32[]{:S(2)}, u32[]{:S(2)}) collective-permute-start(f32[4,2,64,256]{3,2,1,0:T(8,128)S(1)} %get-tuple-element.42), channel_id=1, source_target_pairs={{0,1},{2,3},{4,5},{6,7},{8,9},{10,11},{12,13},{14,15},{16,17},{18,... | collective-permute-start | bytes 1572872 | tf_op jit(solution)/shard_map/ppermute | solution.py:492
  4.9 7.2 %collective-permute-start.1 = (f32[4,2,64,256]{3,2,1,0:T(8,128)S(1)}, f32[4,2,64,256]{3,2,1,0:T(8,128)}, u32[]{:S(2)}, u32[]{:S(2)}) collective-permute-start(f32[4,2,64,256]{3,2,1,0:T(8,128)S(1)} %get-tuple-element.41), channel_id=1, source_target_pairs={{1,2},{3,4},{5,6},{7,8},{9,10},{11,12},{13,14},{15,16},{17,18},{19... | collective-permute-start | bytes 1572872 | tf_op jit(solution)/shard_map/ppermute | solution.py:491
  12.1 13.7 %shard_map.64 = (f32[8,2,512,128]{3,2,1,0:T(8,128)S(1)}, f32[8,4,64,256]{3,2,1,0:T(8,128)S(1)}) custom-call(s32[8]{0:T(128)S(1)} %copy-done.6, f32[8,64,8,256]{3,2,1,0:T(8,128)S(1)} %copy-done.3, bf16[512,512]{1,0:T(8,128)(2,1)S(1)} %copy-done.5, s32[8,3,64,8,256]{4,3,2,1,0:T(8,128)} %refs_6_.3), custom_call_target="tpu_custom_call" | custom-call | flops 40000000 | bytes 40000000 | tf_op jit(solution)/shard_map/pallas_call | solution.py:465
  25.9 1.9 %copy-done = f32[8,2,512,128]{3,2,1,0:T(8,128)} copy-done((f32[8,2,512,128]{3,2,1,0:T(8,128)}, f32[8,2,512,128]{3,2,1,0:T(8,128)S(1)}, u32[]{:S(2)}) %copy-start) | copy-done | bytes 4194328
  27.8 0.5 collective-permute-start.3
  28.4 1.5 collective-permute-done.2.refs_4_
  29.8 1.0 collective-permute-done.3.refs_6_
  30.8 2.2 %copy-done.1 = f32[8,2,512,128]{3,2,1,0:T(8,128)S(1)} copy-done((f32[8,2,512,128]{3,2,1,0:T(8,128)S(1)}, f32[8,2,512,128]{3,2,1,0:T(8,128)}, u32[]{:S(2)}) %copy-start.1) | copy-done | bytes 4194328
  33.0 2.3 %shard_map.65.refs_3_ = f32[2,8,2,64,256]{4,3,2,1,0:T(8,128)S(1)} custom-call(s32[8]{0:T(128)S(1)} %copy-done.6, s32[3]{0:T(128)S(1)} %pad_add_fusion.refs_1_, f32[8,2,512,128]{3,2,1,0:T(8,128)S(1)} %copy-done.1, f32[4,2,64,256]{3,2,1,0:T(8,128)S(1)} %collective-permute-done.refs_3_, f32[4,2,64,256]{3,2,1,0:T(8,128)} %collective-permute-done.2.refs_4_, ...), custom_call_target="tpu_custom_call" | custom-call | flops 40000000 | bytes 40000000 | tf_op jit(solution)/shard_map/pallas_call | solution.py:465
  35.3 0.2 slice_bitcast_fusion
  35.6 4.6 %collective-permute-start.5 = (f32[8,2,64,256]{3,2,1,0:T(8,128)S(1)}, f32[8,2,64,256]{3,2,1,0:T(8,128)S(1)}, u32[]{:S(2)}, u32[]{:S(2)}) collective-permute-start(f32[8,2,64,256]{3,2,1,0:T(8,128)S(1)} %get-tuple-element.35), channel_id=1, source_target_pairs={{1,2},{3,4},{5,6},{7,8},{9,10},{11,12},{13,14},{15,16},{17,18},{19... | collective-permute-start | bytes 3145736 | tf_op jit(solution)/shard_map/ppermute | solution.py:491
  40.2 16.1 %shard_map.66.refs_2_.refs_1_ = f32[8,2,512,128]{3,2,1,0:T(8,128)S(1)} custom-call(s32[8]{0:T(128)S(1)} %copy-done.6, s32[3]{0:T(128)S(1)} %pad_add_fusion.refs_1_, f32[8,2,512,128]{3,2,1,0:T(8,128)S(1)} %copy-done.2, f32[2,8,2,64,256]{4,3,2,1,0:T(8,128)S(1)} %shard_map.65.refs_3_, f32[8,64,8,256]{3,2,1,0:T(8,128)} %refs_4_.2, ...), custom_call_target="tpu_custom_call" | custom-call | flops 40000000 | bytes 40000000 | tf_op jit(solution)/shard_map/pallas_call | solution.py:465
  56.3 4.5 %collective-permute-done.4.refs_3_ = f32[8,2,64,256]{3,2,1,0:T(8,128)S(1)} collective-permute-done((f32[8,2,64,256]{3,2,1,0:T(8,128)S(1)}, f32[8,2,64,256]{3,2,1,0:T(8,128)S(1)}, u32[]{:S(2)}, u32[]{:S(2)}) %collective-permute-start.4) | collective-permute-done | bytes 1048608 | tf_op jit(solution)/shard_map/ppermute | solution.py:492
  60.8 6.7 %collective-permute-done.5.refs_4_ = f32[8,2,64,256]{3,2,1,0:T(8,128)S(1)} collective-permute-done((f32[8,2,64,256]{3,2,1,0:T(8,128)S(1)}, f32[8,2,64,256]{3,2,1,0:T(8,128)S(1)}, u32[]{:S(2)}, u32[]{:S(2)}) %collective-permute-start.5) | collective-permute-done | bytes 1048608 | tf_op jit(solution)/shard_map/ppermute | solution.py:491
  67.5 1.6 %shard_map.67 = (f32[8,2,64,256]{3,2,1,0:T(8,128)S(1)}, f32[8,2,64,256]{3,2,1,0:T(8,128)S(1)}, f32[2,8,2,64,256]{4,3,2,1,0:T(8,128)S(1)}) custom-call(s32[8]{0:T(128)S(1)} %copy-done.6, s32[3]{0:T(128)S(1)} %pad_add_fusion.refs_1_, f32[8,2,512,128]{3,2,1,0:T(8,128)S(1)} %shard_map.66.refs_2_.refs_1_, f32[8,2,64,256]{3,2,1,0:T(8,128)S(1)} %collective-permute-done.4.refs_3_, ...), custom_call_target="tpu_custom_call" | custom-call | flops 40000000 | bytes 40000000 | tf_op jit(solution)/shard_map/pallas_call | solution.py:465
  69.1 0.2 slice_bitcast_fusion.2
  69.4 4.3 %collective-permute-start.7 = (f32[8,2,64,256]{3,2,1,0:T(8,128)S(1)}, f32[8,2,64,256]{3,2,1,0:T(8,128)S(1)}, u32[]{:S(2)}, u32[]{:S(2)}) collective-permute-start(f32[8,2,64,256]{3,2,1,0:T(8,128)S(1)} %get-tuple-element.33), channel_id=1, source_target_pairs={{1,2},{3,4},{5,6},{7,8},{9,10},{11,12},{13,14},{15,16},{17,18},{19... | collective-permute-start | bytes 3145736 | tf_op jit(solution)/shard_map/ppermute | solution.py:491
  73.7 15.3 %shard_map.68.refs_2_ = f32[8,2,512,128]{3,2,1,0:T(8,128)S(1)} custom-call(s32[8]{0:T(128)S(1)} %copy-done.6, f32[8,2,512,128]{3,2,1,0:T(8,128)S(1)} %shard_map.66.refs_2_.refs_1_, f32[8,2,64,256]{3,2,1,0:T(8,128)S(1)} %get-tuple-element.23.refs_2_, f32[8,2,64,256]{3,2,1,0:T(8,128)S(1)} %get-tuple-element.24.refs_3_, bf16[1024,256]{1,0:T(8,128)(2,1)S(1)} %copy-done.4, ...), custom_call_target="tpu_custom_call" | custom-call | flops 40000000 | bytes 40000000 | tf_op jit(solution)/shard_map/pallas_call | solution.py:465
  89.1 4.7 %collective-permute-done.6.refs_3_ = f32[8,2,64,256]{3,2,1,0:T(8,128)S(1)} collective-permute-done((f32[8,2,64,256]{3,2,1,0:T(8,128)S(1)}, f32[8,2,64,256]{3,2,1,0:T(8,128)S(1)}, u32[]{:S(2)}, u32[]{:S(2)}) %collective-permute-start.6) | collective-permute-done | bytes 1048608 | tf_op jit(solution)/shard_map/ppermute | solution.py:492
  93.8 6.4 %collective-permute-done.7.refs_4_ = f32[8,2,64,256]{3,2,1,0:T(8,128)S(1)} collective-permute-done((f32[8,2,64,256]{3,2,1,0:T(8,128)S(1)}, f32[8,2,64,256]{3,2,1,0:T(8,128)S(1)}, u32[]{:S(2)}, u32[]{:S(2)}) %collective-permute-start.7) | collective-permute-done | bytes 1048608 | tf_op jit(solution)/shard_map/ppermute | solution.py:491
  100.2 1.7 %shard_map.69 = f32[8,256,256]{2,1,0:T(8,128)S(1)} custom-call(s32[8]{0:T(128)S(1)} %copy-done.6, s32[3]{0:T(128)S(1)} %pad_add_fusion.refs_1_, f32[8,2,512,128]{3,2,1,0:T(8,128)S(1)} %shard_map.68.refs_2_, f32[8,2,64,256]{3,2,1,0:T(8,128)S(1)} %collective-permute-done.6.refs_3_, f32[8,2,64,256]{3,2,1,0:T(8,128)S(1)} %collective-permute-done.7.refs_4_, ...), custom_call_target="tpu_custom_call" | custom-call | flops 40000000 | bytes 40000000 | tf_op jit(solution)/shard_map/pallas_call | solution.py:465
  102.1 2.6 %collective-permute-done.8 = f32[4,256,256]{2,1,0:T(8,128)S(1)} collective-permute-done((f32[4,256,256]{2,1,0:T(8,128)S(1)}, f32[4,256,256]{2,1,0:T(8,128)S(1)}, u32[]{:S(2)}, u32[]{:S(2)}) %collective-permute-start.8) | collective-permute-done | bytes 1048608 | tf_op jit(solution)/shard_map/ppermute | solution.py:587
  104.8 0.2 slice_add_fusion.1
  105.1 4.3 %collective-permute-start.10 = (f32[4,128,256]{2,1,0:T(8,128)S(1)}, f32[4,128,256]{2,1,0:T(8,128)S(1)}, u32[]{:S(2)}, u32[]{:S(2)}) collective-permute-start(f32[4,128,256]{2,1,0:T(8,128)S(1)} %get-tuple-element.39), channel_id=1, source_target_pairs={{1,2},{3,4},{5,6},{7,8},{9,10},{11,12},{13,14},{15,16},{17,18},{19... | collective-permute-start | bytes 1572872 | tf_op jit(solution)/shard_map/ppermute | solution.py:491
  109.5 16.2 %shard_map.70 = f32[8,64,8,256]{3,2,1,0:T(8,128)S(1)} custom-call(s32[8]{0:T(128)S(1)} %copy-done.6, s32[3]{0:T(128)S(1)} %pad_add_fusion.refs_1_, f32[8,2,512,128]{3,2,1,0:T(8,128)S(1)} %shard_map.68.refs_2_, f32[8,2,64,256]{3,2,1,0:T(8,128)S(1)} %collective-permute-done.6.refs_3_, f32[8,2,64,256]{3,2,1,0:T(8,128)S(1)} %collective-permute-done.7.refs_4_, ...), custom_call_target="tpu_custom_call" | custom-call | flops 40000000 | bytes 40000000 | tf_op jit(solution)/shard_map/pallas_call | solution.py:465
  126.1 0.8 copy_bitcast_fusion
  126.9 3.2 %collective-permute-done.11 = f32[4,64,8,256]{3,2,1,0:T(8,128)S(1)} collective-permute-done((f32[4,64,8,256]{3,2,1,0:T(8,128)S(1)}, f32[4,64,8,256]{3,2,1,0:T(8,128)S(1)}, u32[]{:S(2)}, u32[]{:S(2)}) %collective-permute-start.11) | collective-permute-done | bytes 2097184 | tf_op jit(solution)/shard_map/ppermute | solution.py:607
  130.1 0.6 fusion
  130.8 0.8 collective-permute-start.12
  131.6 24.5 %collective-permute-done.12 = f32[2,64,8,256]{3,2,1,0:T(8,128)S(1)} collective-permute-done((f32[2,64,8,256]{3,2,1,0:T(8,128)S(1)}, f32[2,64,8,256]{3,2,1,0:T(8,128)S(1)}, u32[]{:S(2)}, u32[]{:S(2)}) %collective-permute-start.12) | collective-permute-done | bytes 1048608 | tf_op jit(solution)/shard_map/ppermute | solution.py:613
  156.1 1.1 slice_add_fusion
  (34 shorter events, 1.4 us)
Async XLA Ops:
  2.6 9.5 %copy-start.5 = (bf16[512,512]{1,0:T(8,128)(2,1)S(1)}, bf16[512,512]{1,0:T(8,128)(2,1)}, u32[]{:S(2)}) copy-start(bf16[512,512]{1,0:T(8,128)(2,1)} %constant.49.clone.refs_2_.refs_5_) | copy-start | bytes 1572868
  2.7 9.4 %copy-start.3 = (f32[8,64,8,256]{3,2,1,0:T(8,128)S(1)}, f32[8,64,8,256]{3,2,1,0:T(8,128)}, u32[]{:S(2)}) copy-start(f32[8,64,8,256]{3,2,1,0:T(8,128)} %refs_1_.1) | copy-start | bytes 12582916
  2.7 9.4 %copy-start.6 = (s32[8]{0:T(128)S(1)}, s32[8]{0:T(128)}, u32[]{:S(2)}) copy-start(s32[8]{0:T(128)} %refs_0_.13) | copy-start | bytes 100
  2.9 24.9 %collective-permute-start = (f32[4,2,64,256]{3,2,1,0:T(8,128)S(1)}, f32[4,2,64,256]{3,2,1,0:T(8,128)S(1)}, u32[]{:S(2)}, u32[]{:S(2)}) collective-permute-start(f32[4,2,64,256]{3,2,1,0:T(8,128)S(1)} %get-tuple-element.42), channel_id=1, source_target_pairs={{0,1},{2,3},{4,5},{6,7},{8,9},{10,11},{12,13},{14,15},{16,17},{18,... | collective-permute-start | bytes 1572872 | tf_op jit(solution)/shard_map/ppermute | solution.py:492
  4.9 22.9 %collective-permute-start.1 = (f32[4,2,64,256]{3,2,1,0:T(8,128)S(1)}, f32[4,2,64,256]{3,2,1,0:T(8,128)}, u32[]{:S(2)}, u32[]{:S(2)}) collective-permute-start(f32[4,2,64,256]{3,2,1,0:T(8,128)S(1)} %get-tuple-element.41), channel_id=1, source_target_pairs={{1,2},{3,4},{5,6},{7,8},{9,10},{11,12},{13,14},{15,16},{17,18},{19... | collective-permute-start | bytes 1572872 | tf_op jit(solution)/shard_map/ppermute | solution.py:491
  25.8 1.9 %copy-start = (f32[8,2,512,128]{3,2,1,0:T(8,128)}, f32[8,2,512,128]{3,2,1,0:T(8,128)S(1)}, u32[]{:S(2)}) copy-start(f32[8,2,512,128]{3,2,1,0:T(8,128)S(1)} %get-tuple-element.18.refs_2_) | copy-start | bytes 12582916
  27.8 2.0 %collective-permute-start.2 = (f32[4,2,64,256]{3,2,1,0:T(8,128)S(1)}, f32[4,2,64,256]{3,2,1,0:T(8,128)}, u32[]{:S(2)}, u32[]{:S(2)}) collective-permute-start(f32[4,2,64,256]{3,2,1,0:T(8,128)S(1)} %collective-permute-done.refs_3_), channel_id=1, source_target_pairs={{0,32},{32,0},{64,96},{96,64},{1,33},{33,1},{65,97},{97,65},{2,34}... | collective-permute-start | bytes 1572872 | tf_op jit(solution)/shard_map/ppermute | solution.py:533
  27.8 3.0 %collective-permute-start.3 = (f32[4,2,64,256]{3,2,1,0:T(8,128)}, f32[4,2,64,256]{3,2,1,0:T(8,128)}, u32[]{:S(2)}, u32[]{:S(2)}) collective-permute-start(f32[4,2,64,256]{3,2,1,0:T(8,128)} %collective-permute-done.1.refs_5_), channel_id=1, source_target_pairs={{0,32},{32,0},{64,96},{96,64},{1,33},{33,1},{65,97},{97,65},{2,34}... | collective-permute-start | bytes 1572872 | tf_op jit(solution)/shard_map/ppermute | solution.py:534
  30.8 2.2 %copy-start.1 = (f32[8,2,512,128]{3,2,1,0:T(8,128)S(1)}, f32[8,2,512,128]{3,2,1,0:T(8,128)}, u32[]{:S(2)}) copy-start(f32[8,2,512,128]{3,2,1,0:T(8,128)} %copy-done) | copy-start | bytes 12582916
  35.3 4.9 %copy-start.2 = (f32[8,2,512,128]{3,2,1,0:T(8,128)S(1)}, f32[8,2,512,128]{3,2,1,0:T(8,128)}, u32[]{:S(2)}) copy-start(f32[8,2,512,128]{3,2,1,0:T(8,128)} %copy-done) | copy-start | bytes 12582916
  35.5 25.3 %collective-permute-start.4 = (f32[8,2,64,256]{3,2,1,0:T(8,128)S(1)}, f32[8,2,64,256]{3,2,1,0:T(8,128)S(1)}, u32[]{:S(2)}, u32[]{:S(2)}) collective-permute-start(f32[8,2,64,256]{3,2,1,0:T(8,128)S(1)} %get-tuple-element.36), channel_id=1, source_target_pairs={{0,1},{2,3},{4,5},{6,7},{8,9},{10,11},{12,13},{14,15},{16,17},{18,... | collective-permute-start | bytes 3145736 | tf_op jit(solution)/shard_map/ppermute | solution.py:492
  35.6 31.9 %collective-permute-start.5 = (f32[8,2,64,256]{3,2,1,0:T(8,128)S(1)}, f32[8,2,64,256]{3,2,1,0:T(8,128)S(1)}, u32[]{:S(2)}, u32[]{:S(2)}) collective-permute-start(f32[8,2,64,256]{3,2,1,0:T(8,128)S(1)} %get-tuple-element.35), channel_id=1, source_target_pairs={{1,2},{3,4},{5,6},{7,8},{9,10},{11,12},{13,14},{15,16},{17,18},{19... | collective-permute-start | bytes 3145736 | tf_op jit(solution)/shard_map/ppermute | solution.py:491
  69.1 4.6 %copy-start.4 = (bf16[1024,256]{1,0:T(8,128)(2,1)S(1)}, bf16[1024,256]{1,0:T(8,128)(2,1)}, u32[]{:S(2)}) copy-start(bf16[1024,256]{1,0:T(8,128)(2,1)} %constant.50.clone.refs_4_.refs_5_) | copy-start | bytes 1572868
  69.3 24.5 %collective-permute-start.6 = (f32[8,2,64,256]{3,2,1,0:T(8,128)S(1)}, f32[8,2,64,256]{3,2,1,0:T(8,128)S(1)}, u32[]{:S(2)}, u32[]{:S(2)}) collective-permute-start(f32[8,2,64,256]{3,2,1,0:T(8,128)S(1)} %get-tuple-element.34), channel_id=1, source_target_pairs={{0,1},{2,3},{4,5},{6,7},{8,9},{10,11},{12,13},{14,15},{16,17},{18,... | collective-permute-start | bytes 3145736 | tf_op jit(solution)/shard_map/ppermute | solution.py:492
  69.4 30.8 %collective-permute-start.7 = (f32[8,2,64,256]{3,2,1,0:T(8,128)S(1)}, f32[8,2,64,256]{3,2,1,0:T(8,128)S(1)}, u32[]{:S(2)}, u32[]{:S(2)}) collective-permute-start(f32[8,2,64,256]{3,2,1,0:T(8,128)S(1)} %get-tuple-element.33), channel_id=1, source_target_pairs={{1,2},{3,4},{5,6},{7,8},{9,10},{11,12},{13,14},{15,16},{17,18},{19... | collective-permute-start | bytes 3145736 | tf_op jit(solution)/shard_map/ppermute | solution.py:491
  102.0 2.7 %collective-permute-start.8 = (f32[4,256,256]{2,1,0:T(8,128)S(1)}, f32[4,256,256]{2,1,0:T(8,128)S(1)}, u32[]{:S(2)}, u32[]{:S(2)}) collective-permute-start(f32[4,256,256]{2,1,0:T(8,128)S(1)} %slice.69), channel_id=1, source_target_pairs={{0,32},{32,0},{64,96},{96,64},{1,33},{33,1},{65,97},{97,65},{2,34}... | collective-permute-start | bytes 3145736 | tf_op jit(solution)/shard_map/ppermute | solution.py:587
  105.1 20.6 %collective-permute-start.10 = (f32[4,128,256]{2,1,0:T(8,128)S(1)}, f32[4,128,256]{2,1,0:T(8,128)S(1)}, u32[]{:S(2)}, u32[]{:S(2)}) collective-permute-start(f32[4,128,256]{2,1,0:T(8,128)S(1)} %get-tuple-element.39), channel_id=1, source_target_pairs={{1,2},{3,4},{5,6},{7,8},{9,10},{11,12},{13,14},{15,16},{17,18},{19... | collective-permute-start | bytes 1572872 | tf_op jit(solution)/shard_map/ppermute | solution.py:491
  109.4 16.3 %collective-permute-start.9 = (f32[4,128,256]{2,1,0:T(8,128)S(1)}, f32[4,128,256]{2,1,0:T(8,128)S(1)}, u32[]{:S(2)}, u32[]{:S(2)}) collective-permute-start(f32[4,128,256]{2,1,0:T(8,128)S(1)} %get-tuple-element.40), channel_id=1, source_target_pairs={{0,1},{2,3},{4,5},{6,7},{8,9},{10,11},{12,13},{14,15},{16,17},{18,... | collective-permute-start | bytes 1572872 | tf_op jit(solution)/shard_map/ppermute | solution.py:492
  125.8 4.2 %collective-permute-start.11 = (f32[4,64,8,256]{3,2,1,0:T(8,128)S(1)}, f32[4,64,8,256]{3,2,1,0:T(8,128)S(1)}, u32[]{:S(2)}, u32[]{:S(2)}) collective-permute-start(f32[4,64,8,256]{3,2,1,0:T(8,128)S(1)} %slice.61), channel_id=1, source_target_pairs={{0,32},{32,0},{64,96},{96,64},{1,33},{33,1},{65,97},{97,65},{2,34}... | collective-permute-start | bytes 6291464 | tf_op jit(solution)/shard_map/ppermute | solution.py:607
  130.8 25.3 %collective-permute-start.12 = (f32[2,64,8,256]{3,2,1,0:T(8,128)S(1)}, f32[2,64,8,256]{3,2,1,0:T(8,128)S(1)}, u32[]{:S(2)}, u32[]{:S(2)}) collective-permute-start(f32[2,64,8,256]{3,2,1,0:T(8,128)S(1)} %slice.71), channel_id=1, source_target_pairs={{0,64},{64,0},{32,96},{96,32},{1,65},{65,1},{33,97},{97,33},{2,66}... | collective-permute-start | bytes 3145736 | tf_op jit(solution)/shard_map/ppermute | solution.py:613

commit v4 on v3

--- a/solution.py
+++ b/solution.py
@@ -17,7 +17,7 @@
 GROUPS = 8
 VMEM = 2 * 1024 * 1024
 STREAMING = 40 * 1024 * 1024
-UNROLL = 4
+UNROLL = 8
 STRIDE = 16
 PLUS = {-2: 1.0, -1: -6.0, 0: 3.0, 1: 2.0}
 MINUS = {-1: -2.0, 0: -3.0, 1: 6.0, 2: -1.0}

time: 158 us -> 157 us (level)
  Pallas kernels: 67 us -> 62.7 us
  starting transfers between devices: 24 us -> 26.4 us
    pallas_call x7, Pallas kernels: 67 us -> 62.7 us  [call(): pl.pallas_call(kernel, in_specs=in_specs, out_specs=[pl.BlockSpec(memory_...]
    ppermute x4, starting transfers between devices: 20.3 us -> 22.7 us  [swap(): odd = lax.ppermute(odd, 'tile', both_ways[1])]
  transfers between devices with their start and end apart: 13 -> 13, of which waited for: 9 -> 10; matrix products, arithmetic and copies ran while one was open for 1% -> 1% of each run, Pallas kernels for 39% -> 37%
where the time goes in v4:
time: 157 us; the launch traced here: 156 us
  Pallas kernels  62.7 us (40%)
  waiting for transfers between devices  55.9 us (36%)
  starting transfers between devices  26.4 us (17%)
  local copies, waits for them, and re-layouts  8.38 us (5%)
  other arithmetic  2.4 us (2%)
    pallas_call x7, Pallas kernels, call(): pl.pallas_call(kernel, in_specs=in_specs, out_specs=[pl.BlockSpec(memory_...  62.7 us
    ppermute x1, waiting for transfers between devices, shards(): return sums4[2:] + lax.ppermute(sums4[:2], 'subj', y_pairs)  24.5 us
    ppermute x4, starting transfers between devices, swap(): odd = lax.ppermute(odd, 'tile', both_ways[1])  22.7 us
    ppermute x4, waiting for transfers between devices, swap(): odd = lax.ppermute(odd, 'tile', both_ways[1])  13.2 us
    ppermute x4, waiting for transfers between devices, swap(): even = lax.ppermute(even, 'tile', both_ways[0])  10 us
    unnamed x16, local copies, waits for them, and re-layouts  4.24 us
    ppermute x1, waiting for transfers between devices, shards(): arrived = lax.ppermute(sums[:some], 'subj', core_pairs)  3.15 us
  transfers between devices with their start and end apart: 13, of which 10 were waited for; matrix products, arithmetic and copies ran while one was open for 1% of the time, Pallas kernels for 37%

profile of v4, /device:TPU:2, one launch (start us, length us, event | category | flops | bytes accessed | tf_op | source)
XLA Modules:
  0.0 156.1 jit_solution(12519581022047133670)
XLA Ops:
  0.0 2.6 %constant_dynamic-slice_fusion = (f32[4,64,2,256]{3,2,1,0:T(2,128)S(1)}, f32[4,64,2,256]{3,2,1,0:T(2,128)S(1)}) fusion(f32[8,64,8,256]{3,2,1,0:T(8,128)} %refs_1_.1, s32[]{:T(128)S(6)} %select_n.54, s32[]{:T(128)S(6)} %add.32), kind=kLoop, calls=%fused_computation.18 | loop fusion | bytes 2097160 | tf_op jit(solution)/shard_map/slice | solution.py:519
  2.9 2.0 %collective-permute-start = (f32[4,2,64,256]{3,2,1,0:T(8,128)S(1)}, f32[4,2,64,256]{3,2,1,0:T(8,128)S(1)}, u32[]{:S(2)}, u32[]{:S(2)}) collective-permute-start(f32[4,2,64,256]{3,2,1,0:T(8,128)S(1)} %get-tuple-element.42), channel_id=1, source_target_pairs={{0,1},{2,3},{4,5},{6,7},{8,9},{10,11},{12,13},{14,15},{16,17},{18,... | collective-permute-start | bytes 1572872 | tf_op jit(solution)/shard_map/ppermute | solution.py:492
  4.9 7.2 %collective-permute-start.1 = (f32[4,2,64,256]{3,2,1,0:T(8,128)S(1)}, f32[4,2,64,256]{3,2,1,0:T(8,128)}, u32[]{:S(2)}, u32[]{:S(2)}) collective-permute-start(f32[4,2,64,256]{3,2,1,0:T(8,128)S(1)} %get-tuple-element.41), channel_id=1, source_target_pairs={{1,2},{3,4},{5,6},{7,8},{9,10},{11,12},{13,14},{15,16},{17,18},{19... | collective-permute-start | bytes 1572872 | tf_op jit(solution)/shard_map/ppermute | solution.py:491
  12.1 12.9 %shard_map.64 = (f32[8,2,512,128]{3,2,1,0:T(8,128)S(1)}, f32[8,4,64,256]{3,2,1,0:T(8,128)S(1)}) custom-call(s32[8]{0:T(128)S(1)} %copy-done.6, f32[8,64,8,256]{3,2,1,0:T(8,128)S(1)} %copy-done.3, bf16[512,512]{1,0:T(8,128)(2,1)S(1)} %copy-done.5, s32[8,3,64,8,256]{4,3,2,1,0:T(8,128)} %refs_6_.3), custom_call_target="tpu_custom_call" | custom-call | flops 40000000 | bytes 40000000 | tf_op jit(solution)/shard_map/pallas_call | solution.py:465
  25.0 1.9 %copy-done = f32[8,2,512,128]{3,2,1,0:T(8,128)} copy-done((f32[8,2,512,128]{3,2,1,0:T(8,128)}, f32[8,2,512,128]{3,2,1,0:T(8,128)S(1)}, u32[]{:S(2)}) %copy-start) | copy-done | bytes 4194328
  27.0 0.5 collective-permute-start.3
  27.6 1.5 collective-permute-done.2.refs_4_
  29.0 1.0 collective-permute-done.3.refs_6_
  30.0 2.2 %copy-done.1 = f32[8,2,512,128]{3,2,1,0:T(8,128)S(1)} copy-done((f32[8,2,512,128]{3,2,1,0:T(8,128)S(1)}, f32[8,2,512,128]{3,2,1,0:T(8,128)}, u32[]{:S(2)}) %copy-start.1) | copy-done | bytes 4194328
  32.2 2.3 %shard_map.65.refs_3_ = f32[2,8,2,64,256]{4,3,2,1,0:T(8,128)S(1)} custom-call(s32[8]{0:T(128)S(1)} %copy-done.6, s32[3]{0:T(128)S(1)} %pad_add_fusion.refs_1_, f32[8,2,512,128]{3,2,1,0:T(8,128)S(1)} %copy-done.1, f32[4,2,64,256]{3,2,1,0:T(8,128)S(1)} %collective-permute-done.refs_3_, f32[4,2,64,256]{3,2,1,0:T(8,128)} %collective-permute-done.2.refs_4_, ...), custom_call_target="tpu_custom_call" | custom-call | flops 40000000 | bytes 40000000 | tf_op jit(solution)/shard_map/pallas_call | solution.py:465
  34.5 0.2 slice_bitcast_fusion
  34.8 5.4 %collective-permute-start.5 = (f32[8,2,64,256]{3,2,1,0:T(8,128)S(1)}, f32[8,2,64,256]{3,2,1,0:T(8,128)S(1)}, u32[]{:S(2)}, u32[]{:S(2)}) collective-permute-start(f32[8,2,64,256]{3,2,1,0:T(8,128)S(1)} %get-tuple-element.35), channel_id=1, source_target_pairs={{1,2},{3,4},{5,6},{7,8},{9,10},{11,12},{13,14},{15,16},{17,18},{19... | collective-permute-start | bytes 3145736 | tf_op jit(solution)/shard_map/ppermute | solution.py:491
  40.2 14.9 %shard_map.66.refs_2_.refs_1_ = f32[8,2,512,128]{3,2,1,0:T(8,128)S(1)} custom-call(s32[8]{0:T(128)S(1)} %copy-done.6, s32[3]{0:T(128)S(1)} %pad_add_fusion.refs_1_, f32[8,2,512,128]{3,2,1,0:T(8,128)S(1)} %copy-done.2, f32[2,8,2,64,256]{4,3,2,1,0:T(8,128)S(1)} %shard_map.65.refs_3_, f32[8,64,8,256]{3,2,1,0:T(8,128)} %refs_4_.2, ...), custom_call_target="tpu_custom_call" | custom-call | flops 40000000 | bytes 40000000 | tf_op jit(solution)/shard_map/pallas_call | solution.py:465
  55.1 4.9 %collective-permute-done.4.refs_3_ = f32[8,2,64,256]{3,2,1,0:T(8,128)S(1)} collective-permute-done((f32[8,2,64,256]{3,2,1,0:T(8,128)S(1)}, f32[8,2,64,256]{3,2,1,0:T(8,128)S(1)}, u32[]{:S(2)}, u32[]{:S(2)}) %collective-permute-start.4) | collective-permute-done | bytes 1048608 | tf_op jit(solution)/shard_map/ppermute | solution.py:492
  60.0 6.7 %collective-permute-done.5.refs_4_ = f32[8,2,64,256]{3,2,1,0:T(8,128)S(1)} collective-permute-done((f32[8,2,64,256]{3,2,1,0:T(8,128)S(1)}, f32[8,2,64,256]{3,2,1,0:T(8,128)S(1)}, u32[]{:S(2)}, u32[]{:S(2)}) %collective-permute-start.5) | collective-permute-done | bytes 1048608 | tf_op jit(solution)/shard_map/ppermute | solution.py:491
  66.7 1.6 %shard_map.67 = (f32[8,2,64,256]{3,2,1,0:T(8,128)S(1)}, f32[8,2,64,256]{3,2,1,0:T(8,128)S(1)}, f32[2,8,2,64,256]{4,3,2,1,0:T(8,128)S(1)}) custom-call(s32[8]{0:T(128)S(1)} %copy-done.6, s32[3]{0:T(128)S(1)} %pad_add_fusion.refs_1_, f32[8,2,512,128]{3,2,1,0:T(8,128)S(1)} %shard_map.66.refs_2_.refs_1_, f32[8,2,64,256]{3,2,1,0:T(8,128)S(1)} %collective-permute-done.4.refs_3_, ...), custom_call_target="tpu_custom_call" | custom-call | flops 40000000 | bytes 40000000 | tf_op jit(solution)/shard_map/pallas_call | solution.py:465
  68.3 0.2 slice_bitcast_fusion.2
  68.6 5.1 %collective-permute-start.7 = (f32[8,2,64,256]{3,2,1,0:T(8,128)S(1)}, f32[8,2,64,256]{3,2,1,0:T(8,128)S(1)}, u32[]{:S(2)}, u32[]{:S(2)}) collective-permute-start(f32[8,2,64,256]{3,2,1,0:T(8,128)S(1)} %get-tuple-element.33), channel_id=1, source_target_pairs={{1,2},{3,4},{5,6},{7,8},{9,10},{11,12},{13,14},{15,16},{17,18},{19... | collective-permute-start | bytes 3145736 | tf_op jit(solution)/shard_map/ppermute | solution.py:491
  73.7 14.2 %shard_map.68.refs_2_ = f32[8,2,512,128]{3,2,1,0:T(8,128)S(1)} custom-call(s32[8]{0:T(128)S(1)} %copy-done.6, f32[8,2,512,128]{3,2,1,0:T(8,128)S(1)} %shard_map.66.refs_2_.refs_1_, f32[8,2,64,256]{3,2,1,0:T(8,128)S(1)} %get-tuple-element.23.refs_2_, f32[8,2,64,256]{3,2,1,0:T(8,128)S(1)} %get-tuple-element.24.refs_3_, bf16[1024,256]{1,0:T(8,128)(2,1)S(1)} %copy-done.4, ...), custom_call_target="tpu_custom_call" | custom-call | flops 40000000 | bytes 40000000 | tf_op jit(solution)/shard_map/pallas_call | solution.py:465
  87.9 5.1 %collective-permute-done.6.refs_3_ = f32[8,2,64,256]{3,2,1,0:T(8,128)S(1)} collective-permute-done((f32[8,2,64,256]{3,2,1,0:T(8,128)S(1)}, f32[8,2,64,256]{3,2,1,0:T(8,128)S(1)}, u32[]{:S(2)}, u32[]{:S(2)}) %collective-permute-start.6) | collective-permute-done | bytes 1048608 | tf_op jit(solution)/shard_map/ppermute | solution.py:492
  93.0 6.4 %collective-permute-done.7.refs_4_ = f32[8,2,64,256]{3,2,1,0:T(8,128)S(1)} collective-permute-done((f32[8,2,64,256]{3,2,1,0:T(8,128)S(1)}, f32[8,2,64,256]{3,2,1,0:T(8,128)S(1)}, u32[]{:S(2)}, u32[]{:S(2)}) %collective-permute-start.7) | collective-permute-done | bytes 1048608 | tf_op jit(solution)/shard_map/ppermute | solution.py:491
  99.4 1.7 %shard_map.69 = f32[8,256,256]{2,1,0:T(8,128)S(1)} custom-call(s32[8]{0:T(128)S(1)} %copy-done.6, s32[3]{0:T(128)S(1)} %pad_add_fusion.refs_1_, f32[8,2,512,128]{3,2,1,0:T(8,128)S(1)} %shard_map.68.refs_2_, f32[8,2,64,256]{3,2,1,0:T(8,128)S(1)} %collective-permute-done.6.refs_3_, f32[8,2,64,256]{3,2,1,0:T(8,128)S(1)} %collective-permute-done.7.refs_4_, ...), custom_call_target="tpu_custom_call" | custom-call | flops 40000000 | bytes 40000000 | tf_op jit(solution)/shard_map/pallas_call | solution.py:465
  101.3 2.6 %collective-permute-done.8 = f32[4,256,256]{2,1,0:T(8,128)S(1)} collective-permute-done((f32[4,256,256]{2,1,0:T(8,128)S(1)}, f32[4,256,256]{2,1,0:T(8,128)S(1)}, u32[]{:S(2)}, u32[]{:S(2)}) %collective-permute-start.8) | collective-permute-done | bytes 1048608 | tf_op jit(solution)/shard_map/ppermute | solution.py:587
  103.9 0.2 slice_add_fusion.1
  104.3 5.1 %collective-permute-start.10 = (f32[4,128,256]{2,1,0:T(8,128)S(1)}, f32[4,128,256]{2,1,0:T(8,128)S(1)}, u32[]{:S(2)}, u32[]{:S(2)}) collective-permute-start(f32[4,128,256]{2,1,0:T(8,128)S(1)} %get-tuple-element.39), channel_id=1, source_target_pairs={{1,2},{3,4},{5,6},{7,8},{9,10},{11,12},{13,14},{15,16},{17,18},{19... | collective-permute-start | bytes 1572872 | tf_op jit(solution)/shard_map/ppermute | solution.py:491
  109.5 15.1 %shard_map.70 = f32[8,64,8,256]{3,2,1,0:T(8,128)S(1)} custom-call(s32[8]{0:T(128)S(1)} %copy-done.6, s32[3]{0:T(128)S(1)} %pad_add_fusion.refs_1_, f32[8,2,512,128]{3,2,1,0:T(8,128)S(1)} %shard_map.68.refs_2_, f32[8,2,64,256]{3,2,1,0:T(8,128)S(1)} %collective-permute-done.6.refs_3_, f32[8,2,64,256]{3,2,1,0:T(8,128)S(1)} %collective-permute-done.7.refs_4_, ...), custom_call_target="tpu_custom_call" | custom-call | flops 40000000 | bytes 40000000 | tf_op jit(solution)/shard_map/pallas_call | solution.py:465
  125.0 0.8 copy_bitcast_fusion
  125.9 3.2 %collective-permute-done.11 = f32[4,64,8,256]{3,2,1,0:T(8,128)S(1)} collective-permute-done((f32[4,64,8,256]{3,2,1,0:T(8,128)S(1)}, f32[4,64,8,256]{3,2,1,0:T(8,128)S(1)}, u32[]{:S(2)}, u32[]{:S(2)}) %collective-permute-start.11) | collective-permute-done | bytes 2097184 | tf_op jit(solution)/shard_map/ppermute | solution.py:607
  129.0 0.6 fusion
  129.7 0.8 collective-permute-start.12
  130.5 24.5 %collective-permute-done.12 = f32[2,64,8,256]{3,2,1,0:T(8,128)S(1)} collective-permute-done((f32[2,64,8,256]{3,2,1,0:T(8,128)S(1)}, f32[2,64,8,256]{3,2,1,0:T(8,128)S(1)}, u32[]{:S(2)}, u32[]{:S(2)}) %collective-permute-start.12) | collective-permute-done | bytes 1048608 | tf_op jit(solution)/shard_map/ppermute | solution.py:613
  155.0 1.1 slice_add_fusion
  (34 shorter events, 1.4 us)
Async XLA Ops:
  2.6 9.5 %copy-start.5 = (bf16[512,512]{1,0:T(8,128)(2,1)S(1)}, bf16[512,512]{1,0:T(8,128)(2,1)}, u32[]{:S(2)}) copy-start(bf16[512,512]{1,0:T(8,128)(2,1)} %constant.49.clone.refs_2_.refs_5_) | copy-start | bytes 1572868
  2.7 9.4 %copy-start.3 = (f32[8,64,8,256]{3,2,1,0:T(8,128)S(1)}, f32[8,64,8,256]{3,2,1,0:T(8,128)}, u32[]{:S(2)}) copy-start(f32[8,64,8,256]{3,2,1,0:T(8,128)} %refs_1_.1) | copy-start | bytes 12582916
  2.7 9.4 %copy-start.6 = (s32[8]{0:T(128)S(1)}, s32[8]{0:T(128)}, u32[]{:S(2)}) copy-start(s32[8]{0:T(128)} %refs_0_.13) | copy-start | bytes 100
  2.9 24.1 %collective-permute-start = (f32[4,2,64,256]{3,2,1,0:T(8,128)S(1)}, f32[4,2,64,256]{3,2,1,0:T(8,128)S(1)}, u32[]{:S(2)}, u32[]{:S(2)}) collective-permute-start(f32[4,2,64,256]{3,2,1,0:T(8,128)S(1)} %get-tuple-element.42), channel_id=1, source_target_pairs={{0,1},{2,3},{4,5},{6,7},{8,9},{10,11},{12,13},{14,15},{16,17},{18,... | collective-permute-start | bytes 1572872 | tf_op jit(solution)/shard_map/ppermute | solution.py:492
  4.9 22.1 %collective-permute-start.1 = (f32[4,2,64,256]{3,2,1,0:T(8,128)S(1)}, f32[4,2,64,256]{3,2,1,0:T(8,128)}, u32[]{:S(2)}, u32[]{:S(2)}) collective-permute-start(f32[4,2,64,256]{3,2,1,0:T(8,128)S(1)} %get-tuple-element.41), channel_id=1, source_target_pairs={{1,2},{3,4},{5,6},{7,8},{9,10},{11,12},{13,14},{15,16},{17,18},{19... | collective-permute-start | bytes 1572872 | tf_op jit(solution)/shard_map/ppermute | solution.py:491
  25.0 1.9 %copy-start = (f32[8,2,512,128]{3,2,1,0:T(8,128)}, f32[8,2,512,128]{3,2,1,0:T(8,128)S(1)}, u32[]{:S(2)}) copy-start(f32[8,2,512,128]{3,2,1,0:T(8,128)S(1)} %get-tuple-element.18.refs_2_) | copy-start | bytes 12582916
  27.0 2.0 %collective-permute-start.2 = (f32[4,2,64,256]{3,2,1,0:T(8,128)S(1)}, f32[4,2,64,256]{3,2,1,0:T(8,128)}, u32[]{:S(2)}, u32[]{:S(2)}) collective-permute-start(f32[4,2,64,256]{3,2,1,0:T(8,128)S(1)} %collective-permute-done.refs_3_), channel_id=1, source_target_pairs={{0,32},{32,0},{64,96},{96,64},{1,33},{33,1},{65,97},{97,65},{2,34}... | collective-permute-start | bytes 1572872 | tf_op jit(solution)/shard_map/ppermute | solution.py:533
  27.0 3.0 %collective-permute-start.3 = (f32[4,2,64,256]{3,2,1,0:T(8,128)}, f32[4,2,64,256]{3,2,1,0:T(8,128)}, u32[]{:S(2)}, u32[]{:S(2)}) collective-permute-start(f32[4,2,64,256]{3,2,1,0:T(8,128)} %collective-permute-done.1.refs_5_), channel_id=1, source_target_pairs={{0,32},{32,0},{64,96},{96,64},{1,33},{33,1},{65,97},{97,65},{2,34}... | collective-permute-start | bytes 1572872 | tf_op jit(solution)/shard_map/ppermute | solution.py:534
  30.0 2.2 %copy-start.1 = (f32[8,2,512,128]{3,2,1,0:T(8,128)S(1)}, f32[8,2,512,128]{3,2,1,0:T(8,128)}, u32[]{:S(2)}) copy-start(f32[8,2,512,128]{3,2,1,0:T(8,128)} %copy-done) | copy-start | bytes 12582916
  34.5 5.7 %copy-start.2 = (f32[8,2,512,128]{3,2,1,0:T(8,128)S(1)}, f32[8,2,512,128]{3,2,1,0:T(8,128)}, u32[]{:S(2)}) copy-start(f32[8,2,512,128]{3,2,1,0:T(8,128)} %copy-done) | copy-start | bytes 12582916
  34.7 25.3 %collective-permute-start.4 = (f32[8,2,64,256]{3,2,1,0:T(8,128)S(1)}, f32[8,2,64,256]{3,2,1,0:T(8,128)S(1)}, u32[]{:S(2)}, u32[]{:S(2)}) collective-permute-start(f32[8,2,64,256]{3,2,1,0:T(8,128)S(1)} %get-tuple-element.36), channel_id=1, source_target_pairs={{0,1},{2,3},{4,5},{6,7},{8,9},{10,11},{12,13},{14,15},{16,17},{18,... | collective-permute-start | bytes 3145736 | tf_op jit(solution)/shard_map/ppermute | solution.py:492
  34.8 31.9 %collective-permute-start.5 = (f32[8,2,64,256]{3,2,1,0:T(8,128)S(1)}, f32[8,2,64,256]{3,2,1,0:T(8,128)S(1)}, u32[]{:S(2)}, u32[]{:S(2)}) collective-permute-start(f32[8,2,64,256]{3,2,1,0:T(8,128)S(1)} %get-tuple-element.35), channel_id=1, source_target_pairs={{1,2},{3,4},{5,6},{7,8},{9,10},{11,12},{13,14},{15,16},{17,18},{19... | collective-permute-start | bytes 3145736 | tf_op jit(solution)/shard_map/ppermute | solution.py:491
  68.3 5.4 %copy-start.4 = (bf16[1024,256]{1,0:T(8,128)(2,1)S(1)}, bf16[1024,256]{1,0:T(8,128)(2,1)}, u32[]{:S(2)}) copy-start(bf16[1024,256]{1,0:T(8,128)(2,1)} %constant.50.clone.refs_4_.refs_5_) | copy-start | bytes 1572868
  68.5 24.5 %collective-permute-start.6 = (f32[8,2,64,256]{3,2,1,0:T(8,128)S(1)}, f32[8,2,64,256]{3,2,1,0:T(8,128)S(1)}, u32[]{:S(2)}, u32[]{:S(2)}) collective-permute-start(f32[8,2,64,256]{3,2,1,0:T(8,128)S(1)} %get-tuple-element.34), channel_id=1, source_target_pairs={{0,1},{2,3},{4,5},{6,7},{8,9},{10,11},{12,13},{14,15},{16,17},{18,... | collective-permute-start | bytes 3145736 | tf_op jit(solution)/shard_map/ppermute | solution.py:492
  68.6 30.8 %collective-permute-start.7 = (f32[8,2,64,256]{3,2,1,0:T(8,128)S(1)}, f32[8,2,64,256]{3,2,1,0:T(8,128)S(1)}, u32[]{:S(2)}, u32[]{:S(2)}) collective-permute-start(f32[8,2,64,256]{3,2,1,0:T(8,128)S(1)} %get-tuple-element.33), channel_id=1, source_target_pairs={{1,2},{3,4},{5,6},{7,8},{9,10},{11,12},{13,14},{15,16},{17,18},{19... | collective-permute-start | bytes 3145736 | tf_op jit(solution)/shard_map/ppermute | solution.py:491
  101.2 2.7 %collective-permute-start.8 = (f32[4,256,256]{2,1,0:T(8,128)S(1)}, f32[4,256,256]{2,1,0:T(8,128)S(1)}, u32[]{:S(2)}, u32[]{:S(2)}) collective-permute-start(f32[4,256,256]{2,1,0:T(8,128)S(1)} %slice.69), channel_id=1, source_target_pairs={{0,32},{32,0},{64,96},{96,64},{1,33},{33,1},{65,97},{97,65},{2,34}... | collective-permute-start | bytes 3145736 | tf_op jit(solution)/shard_map/ppermute | solution.py:587
  104.3 20.4 %collective-permute-start.10 = (f32[4,128,256]{2,1,0:T(8,128)S(1)}, f32[4,128,256]{2,1,0:T(8,128)S(1)}, u32[]{:S(2)}, u32[]{:S(2)}) collective-permute-start(f32[4,128,256]{2,1,0:T(8,128)S(1)} %get-tuple-element.39), channel_id=1, source_target_pairs={{1,2},{3,4},{5,6},{7,8},{9,10},{11,12},{13,14},{15,16},{17,18},{19... | collective-permute-start | bytes 1572872 | tf_op jit(solution)/shard_map/ppermute | solution.py:491
  109.4 15.3 %collective-permute-start.9 = (f32[4,128,256]{2,1,0:T(8,128)S(1)}, f32[4,128,256]{2,1,0:T(8,128)S(1)}, u32[]{:S(2)}, u32[]{:S(2)}) collective-permute-start(f32[4,128,256]{2,1,0:T(8,128)S(1)} %get-tuple-element.40), channel_id=1, source_target_pairs={{0,1},{2,3},{4,5},{6,7},{8,9},{10,11},{12,13},{14,15},{16,17},{18,... | collective-permute-start | bytes 1572872 | tf_op jit(solution)/shard_map/ppermute | solution.py:492
  124.8 4.2 %collective-permute-start.11 = (f32[4,64,8,256]{3,2,1,0:T(8,128)S(1)}, f32[4,64,8,256]{3,2,1,0:T(8,128)S(1)}, u32[]{:S(2)}, u32[]{:S(2)}) collective-permute-start(f32[4,64,8,256]{3,2,1,0:T(8,128)S(1)} %slice.61), channel_id=1, source_target_pairs={{0,32},{32,0},{64,96},{96,64},{1,33},{33,1},{65,97},{97,65},{2,34}... | collective-permute-start | bytes 6291464 | tf_op jit(solution)/shard_map/ppermute | solution.py:607
  129.7 25.3 %collective-permute-start.12 = (f32[2,64,8,256]{3,2,1,0:T(8,128)S(1)}, f32[2,64,8,256]{3,2,1,0:T(8,128)S(1)}, u32[]{:S(2)}, u32[]{:S(2)}) collective-permute-start(f32[2,64,8,256]{3,2,1,0:T(8,128)S(1)} %slice.71), channel_id=1, source_target_pairs={{0,64},{64,0},{32,96},{96,32},{1,65},{65,1},{33,97},{97,33},{2,66}... | collective-permute-start | bytes 3145736 | tf_op jit(solution)/shard_map/ppermute | solution.py:613
